TPU v7x, 32 devices: a whole 2x2x4 slice. The times are simulated.
32 devices in a mesh: dp: 16 (over z, y, x), mp: 2 (over core).
Axes of the slice: x: 2, y: 2, z: 4, core: 2. Of those that a mesh axis runs over, the one named last changes fastest.
Arguments:
- tokens: bfloat16 [32768, 512], P('dp'), may hold values from -6 to 6
- seq_starts: int32 [16, 16], P('dp'), may hold values from 0 to 2048, as said below
- seq_lengths: int32 [16, 16], P('dp'), may hold values from 0 to 2048, as said below
- attend_weight: bfloat16 [3, 512, 512], P(None, None, 'mp'), may hold values from -0.25 to 0.25
- attend_bias: float32 [2, 512], P(None, 'mp'), may hold values from -3 to 3
- output_weight: bfloat16 [512, 512], P('mp'), may hold values from -1 to 1
- output_bias: float32 [512], replicated, may hold values from -3 to 3
- first_gain: float32 [512], replicated, may hold values from 0.5 to 1.5
- first_shift: float32 [512], replicated, may hold values from -3 to 3
- expand_weight: bfloat16 [512, 2048], P(None, 'mp'), may hold values from -0.25 to 0.25
- expand_bias: float32 [2048], P('mp'), may hold values from -3 to 3
- reduce_weight: bfloat16 [2048, 512], P('mp'), may hold values from -0.25 to 0.25
- reduce_bias: float32 [512], replicated, may hold values from -3 to 3
- second_gain: float32 [512], replicated, may hold values from 0.5 to 1.5
- second_shift: float32 [512], replicated, may hold values from -3 to 3
- cotangent: bfloat16 [32768, 512], P('dp'), may hold values from -6 to 6
Outputs:
- layer_out: bfloat16 [32768, 512], P('dp')
- grad_tokens: bfloat16 [32768, 512], P('dp')
- grad_attend: float32 [3, 512, 512], P(None, None, 'mp')
- grad_attbias: float32 [2, 512], P(None, 'mp')
- grad_output: float32 [512, 512], P('mp')
- grad_outbias: float32 [512], replicated
- grad_firstgain: float32 [512], replicated
- grad_firstshift: float32 [512], replicated
- grad_expand: float32 [512, 2048], P(None, 'mp')
- grad_expbias: float32 [2048], P('mp')
- grad_reduce: float32 [2048, 512], P('mp')
- grad_redbias: float32 [512], replicated
- grad_secondgain: float32 [512], replicated
- grad_secondshift: float32 [512], replicated
Inputs may be any that keep to these rules, and one draw needn't show every extreme that they name: `seq_starts`: in each device row, used slots come first, sequences stand in order, each ends at or before the next one's start and within 2048; an unused slot has length 0 and start 2048; some device holds a single sequence of 2048 tokens. `seq_lengths`: A used slot has 21 or more tokens, the first 20 being memory tokens; an unused slot has 0; every device holds at least one sequence.
All inputs are finite; a program needn't handle non-finite values.
Results may differ from a plain program's by a relative error of at most 0.014.
The roundings to bfloat16 on the way count: a program that leaves them out, or rounds other values in their place, can miss the bound.
Values sent between devices are 32-bit elements; how exact they have to be, the bound alone decides.
No kernel may reach another device: no remote copies, remote signals or barrier semaphores. Data moves between devices by JAX's collectives and lax.ppermute only.
A program may use at most 128 MiB of HBM per device.

v0:
```python
import jax
import jax.numpy as jnp
from jax import lax
from jax.sharding import PartitionSpec as P

HD = 64


EPS = 1e-05
NEG = -1e30


def segment_ids(starts, lengths, count):
    places = jnp.arange(count, dtype=jnp.int32)[:, None]
    inside = (places >= starts[None, :]) & (places < (starts + lengths)[None, :])
    labels = jnp.arange(1, starts.shape[0] + 1, dtype=jnp.int32)[None, :]
    return jnp.sum(jnp.where(inside, labels, 0), axis=1)


def layer_norm(values, gain, shift):
    center = values - jnp.mean(values, axis=-1, keepdims=True)
    spread = jnp.mean(center * center, axis=-1, keepdims=True)
    return center * lax.rsqrt(spread + EPS) * gain + shift


def exact_gelu(values):
    return jax.nn.gelu(values, approximate=False)


def local(
    tokens,
    seq_starts,
    seq_lengths,
    attend_weight,
    attend_bias,
    output_weight,
    output_bias,
    first_gain,
    first_shift,
    expand_weight,
    expand_bias,
    reduce_weight,
    reduce_bias,
    second_gain,
    second_shift,
    cotangent,
):
    f32 = jnp.float32
    bf16 = jnp.bfloat16
    count = tokens.shape[0]
    local_heads = attend_weight.shape[2] // HD
    block_rows = min(512, count)
    blocks = count // block_rows
    scale = HD ** (-0.5)
    segment = segment_ids(seq_starts[0], seq_lengths[0], count)
    valid = (segment > 0).astype(f32)[:, None]
    rows = tokens.astype(f32)
    bias_full = jnp.stack([attend_bias[0], jnp.zeros_like(attend_bias[0]), attend_bias[1]])
    mixed = (
        jnp.einsum("td,cde->cte", tokens, attend_weight, preferred_element_type=f32)
        + bias_full[:, None, :]
    ).astype(bf16)
    query_all = mixed[0].reshape(count, local_heads, HD)
    key_all = mixed[1].reshape(count, local_heads, HD)
    value_all = mixed[2].reshape(count, local_heads, HD)
    query_blocks = query_all.reshape(blocks, block_rows, local_heads, HD)
    segment_blocks = segment.reshape(blocks, block_rows)

    def block_scores(query_blk, segment_blk):
        scores = jnp.einsum("qhd,khd->hqk", query_blk, key_all, preferred_element_type=f32) * scale
        allowed = (segment_blk[:, None] == segment[None, :])[None]
        return jnp.where(allowed, scores, NEG)

    def forward_block(pair):
        scores = block_scores(pair[0], pair[1])
        peak = jnp.max(scores, axis=-1, keepdims=True)
        total = jnp.sum(jnp.exp(scores - peak), axis=-1, keepdims=True)
        log_total = peak + jnp.log(total)
        probs_low = jnp.exp(scores - log_total).astype(bf16)
        attended = jnp.einsum("hqk,khd->qhd", probs_low, value_all, preferred_element_type=f32)
        return (attended, log_total)

    attended_blocks, log_totals = lax.map(forward_block, (query_blocks, segment_blocks))
    attended = attended_blocks.reshape(count, local_heads * HD).astype(bf16)
    partial_mix = jnp.dot(attended, output_weight, preferred_element_type=f32)
    branch = lax.psum(partial_mix, "mp") + output_bias
    normed, first_back = jax.vjp(layer_norm, rows + branch, first_gain, first_shift)
    normed_low = normed.astype(bf16)
    hidden = jnp.dot(normed_low, expand_weight, preferred_element_type=f32) + expand_bias
    active, gelu_back = jax.vjp(exact_gelu, hidden)
    active_low = active.astype(bf16)
    partial_out = jnp.dot(active_low, reduce_weight, preferred_element_type=f32)
    result = lax.psum(partial_out, "mp") + reduce_bias
    final, second_back = jax.vjp(layer_norm, normed + result, second_gain, second_shift)
    layer_out = (final * valid).astype(bf16)
    grad_resid_two, grad_secondgain, grad_secondshift = second_back(cotangent.astype(f32) * valid)
    grad_result = grad_resid_two.astype(bf16)
    grad_redbias = jnp.sum(grad_result.astype(f32), axis=0)
    grad_reduce = jnp.einsum("tf,td->fd", active_low, grad_result, preferred_element_type=f32)
    grad_active = jnp.einsum("td,fd->tf", grad_result, reduce_weight, preferred_element_type=f32)
    (grad_hidden_full,) = gelu_back(grad_active)
    grad_hidden = grad_hidden_full.astype(bf16)
    grad_expbias = jnp.sum(grad_hidden.astype(f32), axis=0)
    grad_expand = jnp.einsum("td,tf->df", normed_low, grad_hidden, preferred_element_type=f32)
    partial_normed = jnp.einsum("tf,df->td", grad_hidden, expand_weight, preferred_element_type=f32)
    grad_normed = grad_resid_two + lax.psum(partial_normed, "mp")
    grad_resid_one, grad_firstgain, grad_firstshift = first_back(grad_normed)
    grad_branch = grad_resid_one.astype(bf16)
    grad_outbias = jnp.sum(grad_branch.astype(f32), axis=0)
    grad_output = jnp.einsum("te,td->ed", attended, grad_branch, preferred_element_type=f32)
    grad_attended = jnp.einsum(
        "td,ed->te", grad_branch, output_weight, preferred_element_type=f32
    ).astype(bf16)
    grad_blocks = grad_attended.reshape(blocks, block_rows, local_heads, HD)

    def backward_block(carry, item):
        key_grad, value_grad = carry
        query_blk, segment_blk, log_total, grad_blk = item
        probs = jnp.exp(block_scores(query_blk, segment_blk) - log_total)
        probs_low = probs.astype(bf16)
        grad_probs = jnp.einsum("qhd,khd->hqk", grad_blk, value_all, preferred_element_type=f32)
        inner = jnp.sum(probs * grad_probs, axis=-1, keepdims=True)
        grad_scores = (probs * (grad_probs - inner)).astype(bf16)
        query_grad = (
            jnp.einsum("hqk,khd->qhd", grad_scores, key_all, preferred_element_type=f32) * scale
        )
        key_grad = (
            key_grad
            + jnp.einsum("hqk,qhd->khd", grad_scores, query_blk, preferred_element_type=f32) * scale
        )
        value_grad = value_grad + jnp.einsum(
            "hqk,qhd->khd", probs_low, grad_blk, preferred_element_type=f32
        )
        return ((key_grad, value_grad), query_grad)

    zero_grad = jnp.zeros((count, local_heads, HD), f32)
    (key_grad, value_grad), query_grads = lax.scan(
        backward_block,
        (zero_grad, zero_grad),
        (query_blocks, segment_blocks, log_totals, grad_blocks),
    )
    width = local_heads * HD
    grad_mixed = jnp.stack(
        [
            query_grads.reshape(count, width),
            key_grad.reshape(count, width),
            value_grad.reshape(count, width),
        ]
    ).astype(bf16)
    grad_attbias = jnp.stack(
        [jnp.sum(grad_mixed[0].astype(f32), axis=0), jnp.sum(grad_mixed[2].astype(f32), axis=0)]
    )
    grad_attend = jnp.einsum("td,cte->cde", tokens, grad_mixed, preferred_element_type=f32)
    partial_rows = jnp.einsum("cte,cde->td", grad_mixed, attend_weight, preferred_element_type=f32)
    grad_tokens = (grad_resid_one + lax.psum(partial_rows, "mp")).astype(bf16)
    (
        grad_attend,
        grad_attbias,
        grad_output,
        grad_outbias,
        grad_firstgain,
        grad_firstshift,
        grad_expand,
        grad_expbias,
        grad_reduce,
        grad_redbias,
        grad_secondgain,
        grad_secondshift,
    ) = lax.psum(
        (
            grad_attend,
            grad_attbias,
            grad_output,
            grad_outbias,
            grad_firstgain,
            grad_firstshift,
            grad_expand,
            grad_expbias,
            grad_reduce,
            grad_redbias,
            grad_secondgain,
            grad_secondshift,
        ),
        "dp",
    )
    return (
        layer_out,
        grad_tokens,
        grad_attend,
        grad_attbias,
        grad_output,
        grad_outbias,
        grad_firstgain,
        grad_firstshift,
        grad_expand,
        grad_expbias,
        grad_reduce,
        grad_redbias,
        grad_secondgain,
        grad_secondshift,
    )


def solution(mesh):
    return jax.shard_map(
        local,
        mesh=mesh,
        in_specs=(
            P("dp", None),
            P("dp", None),
            P("dp", None),
            P(None, None, "mp"),
            P(None, "mp"),
            P("mp", None),
            P(),
            P(),
            P(),
            P(None, "mp"),
            P("mp"),
            P("mp", None),
            P(),
            P(),
            P(),
            P("dp", None),
        ),
        out_specs=(
            P("dp", None),
            P("dp", None),
            P(None, None, "mp"),
            P(None, "mp"),
            P("mp", None),
            P(),
            P(),
            P(),
            P(None, "mp"),
            P("mp"),
            P("mp", None),
            P(),
            P(),
            P(),
        ),
        check_vma=False,
    )
```

profile of v0, /device:TPU:0, one launch (start us, length us, event | category | flops | bytes accessed | tf_op | source)
XLA Modules:
  0.0 739.2 jit_solution(10153203732775457311)
XLA Ops:
  21.0 61.3 %while.27 = (s32[]{:T(128)}, bf16[4,512,4,64]{1,3,2,0:T(8,128)(2,1)}, f32[4,4,512,1]{2,1,3,0:T(4,128)}, s32[4,512]{1,0:T(4,128)S(1)}, s32[2048]{0:T(1024)S(1)}, ...) while((s32[]{:T(128)}, ...), condition=%wide.region_4.5_spmd, body=%wide.region_1.4_spmd.sunk | while | flops 1120925696 | bytes 65878188 | solution.py:83
  21.7 4.4 fusion.122
  26.1 4.3 exponential_reduce_fusion.2
  31.1 4.3 fusion.123
  37.0 4.4 fusion.122
  41.5 4.3 exponential_reduce_fusion.2
  46.4 4.3 fusion.123
  52.3 4.4 fusion.122
  56.8 4.3 exponential_reduce_fusion.2
  61.8 4.3 fusion.123
  67.7 4.4 fusion.122
  72.1 4.3 exponential_reduce_fusion.2
  77.1 4.3 fusion.123
  88.5 12.9 %all-reduce.10.cloned.1.call-start = ((), (), s32[]{:S(2)}) async-start(), calls=%async_computation.1 | async-start | bytes 8388608 | tf_op jit(solution)/shard_map/psum | solution.py:93
  101.4 18.3 %all-reduce.8.cloned.1.call-done = f32[2048,512]{1,0:T(8,128)} async-done(((f32[2048,512]{1,0:T(8,128)}), f32[2048,512]{1,0:T(8,128)}) %all-reduce.8.cloned.1.call-update) | async-done | bytes 4194320 | tf_op jit(solution)/shard_map/psum | solution.py:86
  124.2 22.5 %multiply_convert_fusion.1 = (bf16[2048,1024]{1,0:T(8,128)(2,1)S(1)}, f32[2048,1024]{1,0:T(8,128)}, f32[2048,1024]{1,0:T(8,128)}) fusion(f32[1024]{0:T(1024)S(1)} %copy-done.57, bf16[512,1024]{1,0:T(8,128)(2,1)S(1)} %copy-done, f32[2048,512]{1,0:T(8,128)S(1)} %get-tuple-element.330, f32[512]{0:T(512)S(1)} %copy-done.53, f32[512]{0:T(512)S(1)} %copy-done.40, ...), kind=kOutput, calls=%fused_computation.55 | convolution fusion | flops 2291138560 | bytes 26238976 | tf_op jit(solution)/shard_map/dot_general | solution.py:89
  148.7 4.4 fusion.74
  153.2 29.7 %all-reduce.10.cloned.1.call-done = f32[2048,512]{1,0:T(8,128)} async-done(((f32[2048,512]{1,0:T(8,128)}), f32[2048,512]{1,0:T(8,128)}) %all-reduce.10.cloned.1.call-update) | async-done | bytes 4194320 | tf_op jit(solution)/shard_map/psum | solution.py:93
  197.8 9.1 %convert_reduce_fusion = (f32[1024]{0:T(1024)}, bf16[2048,1024]{1,0:T(8,128)(2,1)S(1)}) fusion(f32[2048,1024]{1,0:T(8,128)S(1)} %bitcast.154, bf16[2048,512]{1,0:T(8,128)(2,1)S(1)} %get-tuple-element.315, bf16[1024,512]{1,0:T(8,128)(2,1)S(1)} %copy-done.56, f32[2048,1024]{1,0:T(8,128)} %get-tuple-element.341, f32[1024]{0:T(1024)S(1)} %copy-done.57), kind=kOutput, calls=%fused_computation.53 | convolution fusion | flops 2183134208 | bytes 24125440 | tf_op jit(solution)/shard_map/td,fd->tf/dot_general | solution.py:100
  208.9 4.4 fusion.75
  213.3 29.7 %all-reduce.12.cloned.1.call-done = f32[2048,512]{1,0:T(8,128)} async-done(((f32[2048,512]{1,0:T(8,128)}), f32[2048,512]{1,0:T(8,128)}) %all-reduce.12.cloned.1.call-update) | async-done | bytes 4194320 | tf_op jit(solution)/shard_map/psum | solution.py:106
  243.1 6.3 multiply_reduce_fusion.2
  263.1 189.4 %while.28 = (s32[]{:T(128)}, f32[2048,4,64]{0,2,1:T(8,128)}, f32[2048,4,64]{0,2,1:T(8,128)}, bf16[4,512,4,64]{1,3,2,0:T(8,128)(2,1)}, bf16[4,512,4,64]{1,3,2,0:T...) while((s32[]{:T(128)}, f32[2048,4,64]{0,2,1:T(8,128)}, ...), condition=%wide.region_18.19_spmd.clone, body=%wide.region_16.18_spmd.clone.sunk | while | flops 2751068160 | bytes 193665456 | solution.py:137
  269.3 7.2 fusion.135
  276.5 11.3 %multiply_reduce_fusion.8 = (f32[4,512]{1,0:T(4,128)}, f32[4,512,2048]{2,1,0:T(8,128)}) fusion(f32[4,512,2048]{2,1,0:T(8,128)S(1)} %fusion.133, f32[4,512]{1,0:T(4,128)S(1)} %dynamic-slice_bitcast_fusion.2, pred[512,2048]{1,0:T(8,128)(4,1)S(1)} %broadcast_compare_fusion.5, bf16[2048,4,64]{0,2,1:T(8,128)(2,1)} %copy-done.10, ...), kind=kOutput, calls=%fused_computation.19.clone.1 | convolution fusion | flops 557840384 | bytes 35930116 | tf_op jit(solution)/shard_map/while/body/eval_jaxpr/qhd,khd->hqk/dot_general | solution.py:121
  287.8 10.9 %multiply_convert_fusion.4 = bf16[4,512,2048]{2,1,0:T(8,128)(2,1)} fusion(f32[4,512,2048]{2,1,0:T(8,128)} %get-tuple-element.470, f32[4,512,2048]{2,1,0:T(8,128)S(1)} %fusion.133, f32[4,512]{1,0:T(4,128)} %get-tuple-element.471, f32[4,512]{1,0:T(4,128)S(1)} %dynamic-slice_bitcast_fusion.2, pred[512,2048]{1,0:T(8,128)(4,1)S(1)} %broadcast_compare_fusion.5), kind=kLoop, calls=%fused_computation.18.clone.1 | loop fusion | flops 25165824 | bytes 43008000 | tf_op jit(solution)/shard_map/while/body/eval_jaxpr/convert_element_type | solution.py:123
  298.7 7.1 fusion.136
  315.6 7.6 %fusion.135 = f32[2048,4,64]{0,2,1:T(8,128)} fusion(f32[4,512,2048]{2,1,0:T(8,128)S(1)} %fusion.133, f32[4,512]{1,0:T(4,128)S(1)} %dynamic-slice_bitcast_fusion.2, pred[512,2048]{1,0:T(8,128)(4,1)S(1)} %broadcast_compare_fusion.5, f32[2048,4,64]{0,2,1:T(8,128)} %get-tuple-element.514, pred[]{:T(512)S(6)} %compare.3, ...), kind=kOutput, calls=%fused_computation.28.clone.1 | convolution fusion | flops 554696704 | bytes 22290436 | tf_op jit(solution)/shard_map/while/body/eval_jaxpr/hqk,qhd->khd/dot_general | solution.py:131
  323.3 11.3 %multiply_reduce_fusion.8 = (f32[4,512]{1,0:T(4,128)}, f32[4,512,2048]{2,1,0:T(8,128)}) fusion(f32[4,512,2048]{2,1,0:T(8,128)S(1)} %fusion.133, f32[4,512]{1,0:T(4,128)S(1)} %dynamic-slice_bitcast_fusion.2, pred[512,2048]{1,0:T(8,128)(4,1)S(1)} %broadcast_compare_fusion.5, bf16[2048,4,64]{0,2,1:T(8,128)(2,1)} %copy-done.10, ...), kind=kOutput, calls=%fused_computation.19.clone.1 | convolution fusion | flops 557840384 | bytes 35930116 | tf_op jit(solution)/shard_map/while/body/eval_jaxpr/qhd,khd->hqk/dot_general | solution.py:121
  334.6 10.9 %multiply_convert_fusion.4 = bf16[4,512,2048]{2,1,0:T(8,128)(2,1)} fusion(f32[4,512,2048]{2,1,0:T(8,128)} %get-tuple-element.470, f32[4,512,2048]{2,1,0:T(8,128)S(1)} %fusion.133, f32[4,512]{1,0:T(4,128)} %get-tuple-element.471, f32[4,512]{1,0:T(4,128)S(1)} %dynamic-slice_bitcast_fusion.2, pred[512,2048]{1,0:T(8,128)(4,1)S(1)} %broadcast_compare_fusion.5), kind=kLoop, calls=%fused_computation.18.clone.1 | loop fusion | flops 25165824 | bytes 43008000 | tf_op jit(solution)/shard_map/while/body/eval_jaxpr/convert_element_type | solution.py:123
  345.5 7.1 fusion.136
  352.6 4.8 fusion.134
  363.1 7.6 %fusion.135 = f32[2048,4,64]{0,2,1:T(8,128)} fusion(f32[4,512,2048]{2,1,0:T(8,128)S(1)} %fusion.133, f32[4,512]{1,0:T(4,128)S(1)} %dynamic-slice_bitcast_fusion.2, pred[512,2048]{1,0:T(8,128)(4,1)S(1)} %broadcast_compare_fusion.5, f32[2048,4,64]{0,2,1:T(8,128)} %get-tuple-element.514, pred[]{:T(512)S(6)} %compare.3, ...), kind=kOutput, calls=%fused_computation.28.clone.1 | convolution fusion | flops 554696704 | bytes 22290436 | tf_op jit(solution)/shard_map/while/body/eval_jaxpr/hqk,qhd->khd/dot_general | solution.py:131
  370.8 11.3 %multiply_reduce_fusion.8 = (f32[4,512]{1,0:T(4,128)}, f32[4,512,2048]{2,1,0:T(8,128)}) fusion(f32[4,512,2048]{2,1,0:T(8,128)S(1)} %fusion.133, f32[4,512]{1,0:T(4,128)S(1)} %dynamic-slice_bitcast_fusion.2, pred[512,2048]{1,0:T(8,128)(4,1)S(1)} %broadcast_compare_fusion.5, bf16[2048,4,64]{0,2,1:T(8,128)(2,1)} %copy-done.10, ...), kind=kOutput, calls=%fused_computation.19.clone.1 | convolution fusion | flops 557840384 | bytes 35930116 | tf_op jit(solution)/shard_map/while/body/eval_jaxpr/qhd,khd->hqk/dot_general | solution.py:121
  382.1 10.9 %multiply_convert_fusion.4 = bf16[4,512,2048]{2,1,0:T(8,128)(2,1)} fusion(f32[4,512,2048]{2,1,0:T(8,128)} %get-tuple-element.470, f32[4,512,2048]{2,1,0:T(8,128)S(1)} %fusion.133, f32[4,512]{1,0:T(4,128)} %get-tuple-element.471, f32[4,512]{1,0:T(4,128)S(1)} %dynamic-slice_bitcast_fusion.2, pred[512,2048]{1,0:T(8,128)(4,1)S(1)} %broadcast_compare_fusion.5), kind=kLoop, calls=%fused_computation.18.clone.1 | loop fusion | flops 25165824 | bytes 43008000 | tf_op jit(solution)/shard_map/while/body/eval_jaxpr/convert_element_type | solution.py:123
  393.0 7.1 fusion.136
  400.1 4.8 fusion.134
  410.6 7.6 %fusion.135 = f32[2048,4,64]{0,2,1:T(8,128)} fusion(f32[4,512,2048]{2,1,0:T(8,128)S(1)} %fusion.133, f32[4,512]{1,0:T(4,128)S(1)} %dynamic-slice_bitcast_fusion.2, pred[512,2048]{1,0:T(8,128)(4,1)S(1)} %broadcast_compare_fusion.5, f32[2048,4,64]{0,2,1:T(8,128)} %get-tuple-element.514, pred[]{:T(512)S(6)} %compare.3, ...), kind=kOutput, calls=%fused_computation.28.clone.1 | convolution fusion | flops 554696704 | bytes 22290436 | tf_op jit(solution)/shard_map/while/body/eval_jaxpr/hqk,qhd->khd/dot_general | solution.py:131
  418.2 11.3 %multiply_reduce_fusion.8 = (f32[4,512]{1,0:T(4,128)}, f32[4,512,2048]{2,1,0:T(8,128)}) fusion(f32[4,512,2048]{2,1,0:T(8,128)S(1)} %fusion.133, f32[4,512]{1,0:T(4,128)S(1)} %dynamic-slice_bitcast_fusion.2, pred[512,2048]{1,0:T(8,128)(4,1)S(1)} %broadcast_compare_fusion.5, bf16[2048,4,64]{0,2,1:T(8,128)(2,1)} %copy-done.10, ...), kind=kOutput, calls=%fused_computation.19.clone.1 | convolution fusion | flops 557840384 | bytes 35930116 | tf_op jit(solution)/shard_map/while/body/eval_jaxpr/qhd,khd->hqk/dot_general | solution.py:121
  429.6 10.9 %multiply_convert_fusion.4 = bf16[4,512,2048]{2,1,0:T(8,128)(2,1)} fusion(f32[4,512,2048]{2,1,0:T(8,128)} %get-tuple-element.470, f32[4,512,2048]{2,1,0:T(8,128)S(1)} %fusion.133, f32[4,512]{1,0:T(4,128)} %get-tuple-element.471, f32[4,512]{1,0:T(4,128)S(1)} %dynamic-slice_bitcast_fusion.2, pred[512,2048]{1,0:T(8,128)(4,1)S(1)} %broadcast_compare_fusion.5), kind=kLoop, calls=%fused_computation.18.clone.1 | loop fusion | flops 25165824 | bytes 43008000 | tf_op jit(solution)/shard_map/while/body/eval_jaxpr/convert_element_type | solution.py:123
  440.5 7.1 fusion.136
  447.6 4.8 fusion.134
  465.5 5.6 convolution_bitcast_fusion
  472.6 6.0 fusion.77
  478.8 6.7 fusion.62
  490.8 80.3 %all-reduce = (f32[2,256]{1,0:T(2,128)}, f32[512]{0:T(512)}, f32[512]{0:T(512)}, f32[512]{0:T(512)}, f32[1024]{0:T(1024)}, /*index=5*/f32[512]{0:T(512)}, f32[512]{0:T(512)}, f32[512]{0:T(512)}) all-reduce(f32[2,256]{1,0:T(2,128)S(1)} %pad_maximum_fusion.4, f32[512]{0:T(512)S(1)} %copy-done.48, ...), channel_id=1, replica_groups=mesh['dp'=16,'mp'=2] {'dp'}, use_global_device_ids=true, to_apply=%region_23.24 | all-reduce | flops 4608 | bytes 36864 | tf_op jit(solution)/shard_map/psum | solution.py:169
  571.0 5.2 add_convert_fusion.2
  576.3 146.6 %all-reduce.16.cloned.1.call-done = (f32[3,512,256]{1,2,0:T(8,128)}, f32[256,512]{1,0:T(8,128)}, f32[512,1024]{1,0:T(8,128)}, f32[1024,512]{1,0:T(8,128)}) async-done(((f32[3,512,256]{1,2,0:T(8,128)}, f32[256,512]{1,0:T(8,128)}, f32[512,1024]{1,0:T(8,128)}, f32[1024,512]{1,0:T(8,128)}), (f32[3,512,256]{1,2,0:T(8,128)}, f32[256,512]{1,0:T(8,128)}, f32[512,1024]{1,0:T(8,128)}, ...) | async-done | bytes 6291472 | tf_op jit(solution)/shard_map/psum | solution.py:169
  (283 shorter events, 121.9 us)
Async XLA Ops:
  7.2 117.0 %copy-start = (bf16[512,1024]{1,0:T(8,128)(2,1)S(1)}, bf16[512,1024]{1,0:T(8,128)(2,1)}, u32[]{:S(2)}) copy-start(bf16[512,1024]{1,0:T(8,128)(2,1)} %param.29) | copy-start | bytes 3145732
  7.2 112.5 %all-reduce.8.cloned.1.call-start = ((), (), s32[]{:S(2)}) async-start(), calls=%async_computation | async-start | bytes 8388608 | tf_op jit(solution)/shard_map/psum | solution.py:86
  26.1 5.0 copy-start.21
  41.5 5.0 copy-start.21
  56.8 5.0 copy-start.21
  72.1 5.0 copy-start.21
  88.4 31.3 %copy-start.50 = (f32[512]{0:T(512)S(1)}, f32[512]{0:T(512)}, u32[]{:S(2)}) copy-start(f32[512]{0:T(512)} %param.26) | copy-start | bytes 6148
  88.5 94.4 %all-reduce.10.cloned.1.call-start = ((), (), s32[]{:S(2)}) async-start(), calls=%async_computation.1 | async-start | bytes 8388608 | tf_op jit(solution)/shard_map/psum | solution.py:93
  123.2 23.5 %copy-start.5 = (f32[2048,512]{1,0:T(8,128)}, f32[2048,512]{1,0:T(8,128)S(1)}, u32[]{:S(2)}) copy-start(f32[2048,512]{1,0:T(8,128)S(1)} %get-tuple-element.330) | copy-start | bytes 12582916
  123.3 126.1 %copy-start.32 = (f32[2048]{0:T(1024)}, f32[2048]{0:T(1024)S(1)}, u32[]{:S(2)}) copy-start(f32[2048]{0:T(1024)S(1)} %broadcast_multiply_fusion.1) | copy-start | bytes 24580
  124.2 125.2 %copy-start.34 = (f32[2048]{0:T(1024)}, f32[2048]{0:T(1024)S(1)}, u32[]{:S(2)}) copy-start(f32[2048]{0:T(1024)S(1)} %fusion.58) | copy-start | bytes 24580
  124.2 24.5 %copy-start.55 = (bf16[1024,512]{1,0:T(8,128)(2,1)S(1)}, bf16[1024,512]{1,0:T(8,128)(2,1)}, u32[]{:S(2)}) copy-start(bf16[1024,512]{1,0:T(8,128)(2,1)} %param.31) | copy-start | bytes 3145732
  153.1 29.8 %copy-start.52 = (f32[512]{0:T(512)S(1)}, f32[512]{0:T(512)}, u32[]{:S(2)}) copy-start(f32[512]{0:T(512)} %param.32) | copy-start | bytes 6148
  153.1 89.9 %all-reduce.12.cloned.1.call-start = ((), (), s32[]{:S(2)}) async-start(), calls=%async_computation.2 | async-start | bytes 8388608 | tf_op jit(solution)/shard_map/psum | solution.py:106
  191.1 6.6 slice-start
  191.1 6.6 slice-start.1
  197.7 9.2 %copy-start.16 = (bf16[2048,512]{1,0:T(8,128)(2,1)}, bf16[2048,512]{1,0:T(8,128)(2,1)S(1)}, u32[]{:S(2)}) copy-start(bf16[2048,512]{1,0:T(8,128)(2,1)S(1)} %get-tuple-element.315) | copy-start | bytes 6291460
  213.3 357.8 %all-reduce.14.cloned.1.call-start = ((), (), s32[]{:S(2)}) async-start(), calls=%async_computation.3 | async-start | bytes 8388608 | tf_op jit(solution)/shard_map/psum | solution.py:155
  243.0 6.4 copy-start.6
  251.1 5.1 copy-start.38
  298.7 7.1 copy-start.2
  345.5 7.1 copy-start.2
  352.6 4.8 copy-start.11
  352.6 4.8 copy-start.26
  352.6 4.8 copy-start.37
  393.0 7.1 copy-start.2
  400.1 4.8 copy-start.26
  400.1 4.8 copy-start.37
  440.4 7.1 copy-start.2
  447.6 4.8 copy-start.26
  447.6 4.8 copy-start.37
  452.6 6.3 copy-start.8
  460.0 5.4 copy-start.27
  471.1 7.6 %copy-start.33 = (f32[2048]{0:T(1024)S(1)}, f32[2048]{0:T(1024)}, u32[]{:S(2)}) copy-start(f32[2048]{0:T(1024)} %copy-done.32) | copy-start | bytes 24580
  471.1 7.6 %copy-start.35 = (f32[2048]{0:T(1024)S(1)}, f32[2048]{0:T(1024)}, u32[]{:S(2)}) copy-start(f32[2048]{0:T(1024)} %copy-done.34) | copy-start | bytes 24580
  471.1 7.6 %copy-start.41 = (f32[512]{0:T(512)S(1)}, f32[512]{0:T(512)}, u32[]{:S(2)}) copy-start(f32[512]{0:T(512)} %param.27) | copy-start | bytes 6148
  471.1 7.6 %copy-start.54 = (f32[512]{0:T(512)S(1)}, f32[512]{0:T(512)}, u32[]{:S(2)}) copy-start(f32[512]{0:T(512)} %param.28) | copy-start | bytes 6148
  471.1 251.8 %all-reduce.16.cloned.1.call-start = ((), (), s32[]{:S(2)}) async-start(), calls=%async_computation.4 | async-start | bytes 12582912 | tf_op jit(solution)/shard_map/psum | solution.py:169
  472.6 6.1 copy-start.7
  478.7 6.8 copy-start.15
  478.7 6.8 copy-start.19
  478.7 8.2 %copy-start.23 = (bf16[2048,512]{1,0:T(8,128)(2,1)S(1)}, bf16[2048,512]{1,0:T(8,128)(2,1)}, u32[]{:S(2)}) copy-start(bf16[2048,512]{1,0:T(8,128)(2,1)} %param.20) | copy-start | bytes 6291460
  478.7 8.2 %copy-start.28 = (bf16[1,2048,256]{2,1,0:T(8,128)(2,1)S(1)}, bf16[1,2048,256]{2,1,0:T(8,128)(2,1)}, u32[]{:S(2)}) copy-start(bf16[1,2048,256]{2,1,0:T(8,128)(2,1)} %copy.58) | copy-start | bytes 3145732
  478.8 8.2 %copy-start.29 = (bf16[1,2048,256]{2,1,0:T(8,128)(2,1)S(1)}, bf16[1,2048,256]{2,1,0:T(8,128)(2,1)}, u32[]{:S(2)}) copy-start(bf16[1,2048,256]{2,1,0:T(8,128)(2,1)} %copy.59) | copy-start | bytes 3145732
  478.8 8.2 %copy-start.30 = (bf16[1,2048,256]{2,1,0:T(8,128)(2,1)S(1)}, bf16[1,2048,256]{2,1,0:T(8,128)(2,1)}, u32[]{:S(2)}) copy-start(bf16[1,2048,256]{2,1,0:T(8,128)(2,1)} %copy.60) | copy-start | bytes 3145732
  490.0 81.0 %copy-start.39 = (f32[2048]{0:T(1024)S(1)}, f32[2048]{0:T(1024)}, u32[]{:S(2)}) copy-start(f32[2048]{0:T(1024)} %copy-done.38) | copy-start | bytes 24580
  722.9 8.3 %copy-start.24 = (f32[1024,512]{1,0:T(8,128)S(1)}, f32[1024,512]{1,0:T(8,128)}, u32[]{:S(2)}) copy-start(f32[1024,512]{1,0:T(8,128)} %get-tuple-element.548) | copy-start | bytes 6291460
  726.1 6.4 copy-start.1
  (51 other events, 96.8 us)
Sparse Core Ops, SparseCore 0:
  88.6 31.1 all-reduce.7
  153.2 29.5 all-reduce.9
  213.4 29.6 all-reduce.11
  471.2 29.5 all-reduce.13
  508.2 214.5 all-reduce.15
where the time goes:
time: 748 us; the launch traced here: 739 us
  matrix products  242 us (32%)
  waiting for transfers between devices  224 us (30%)
  other arithmetic  104 us (14%)
  blocking collectives  80.3 us (11%)
  local copies, waits for them, and re-layouts  59.6 us (8%)
  between operations  14.5 us (2%)
  starting transfers between devices  13.1 us (2%)
    psum x1, waiting for transfers between devices, local(): lax.psum((grad_attend, grad_attbias, grad_output, grad_outbias, grad_firs...  147 us
    psum x1, blocking collectives, local(): lax.psum((grad_attend, grad_attbias, grad_output, grad_outbias, grad_firs...  80.3 us
    dot_general x4, matrix products, backward_block(): jnp.einsum('qhd,khd->hqk', grad_blk, value_all, preferred_element_type=f32)  45.2 us
    convert_element_type x4, other arithmetic, backward_block(): grad_scores = (probs * (grad_probs - inner)).astype(bf16)  43.6 us
    dot_general x8, matrix products, block_scores(): jnp.einsum('qhd,khd->hqk', query_blk, key_all, preferred_element_type=f32)  32.5 us
    dot_general x4, matrix products, backward_block(): jnp.einsum('hqk,qhd->khd', probs_low, grad_blk, preferred_element_type=f32)  30.1 us
    psum x1, waiting for transfers between devices, local(): grad_normed = grad_resid_two + lax.psum(partial_normed, 'mp')  29.7 us
    psum x1, waiting for transfers between devices, local(): result = lax.psum(partial_out, 'mp') + reduce_bias  29.7 us
  transfers between devices with their start and end apart: 5, of which 4 were waited for; matrix products, arithmetic and copies ran while one was open for 3% of the time, Pallas kernels for 0%

commit v1 on v0

v1 whole, which is shorter than its diff:
```python
import functools
import math

import jax
import jax.numpy as jnp
from jax import lax
from jax.experimental import pallas as pl
from jax.experimental.pallas import tpu as pltpu
from jax.sharding import PartitionSpec as P

HD = 64
EPS = 1e-05
FAR = 1e30
f32 = jnp.float32
bf16 = jnp.bfloat16
QB = 256
LIMIT = 60 * 2**20


def dot(a, b, ca=1, cb=0):
    return lax.dot_general(a, b, (((ca,), (cb,)), ((), ())), preferred_element_type=f32)


def vmem():
    return pl.BlockSpec(memory_space=pltpu.VMEM)


def shape(dims, kind=f32):
    return jax.ShapeDtypeStruct(dims, kind)


def call(body, outs, **extra):
    return pl.pallas_call(
        body,
        out_shape=outs,
        compiler_params=pltpu.CompilerParams(vmem_limit_bytes=LIMIT),
        **extra,
    )


def widen_kernel(*refs):
    count = len(refs) // 2
    for src, dst in zip(refs[:count], refs[count:]):
        dst[...] = src[...].astype(f32)


def widen(*arrays):
    return call(widen_kernel, [shape(a.shape) for a in arrays])(*arrays)


def split3(v):
    high = v.astype(bf16)
    rest = v - high.astype(f32)
    mid = rest.astype(bf16)
    low = (rest - mid.astype(f32)).astype(bf16)
    return high, mid, low


def query_rows(start_col, end_col, base, count):
    slots = start_col.shape[0]
    place = lax.broadcasted_iota(jnp.int32, (slots, count), 1) + base
    inside = jnp.where((place >= start_col) & (place < end_col), 1.0, 0.0)
    alone = 1.0 - jnp.sum(inside, axis=0, keepdims=True)
    return jnp.concatenate([inside, alone], axis=0) * -FAR


def key_columns(start_row, end_row, base, count, slots):
    place = lax.broadcasted_iota(jnp.int32, (count, 128), 0) + base
    lane = lax.broadcasted_iota(jnp.int32, (count, 128), 1)
    inside = jnp.where((place >= start_row) & (place < end_row), 1.0, 0.0)
    used = jnp.sum(inside, axis=1, keepdims=True)
    ones = (lane > slots) & (lane < slots + 4)
    return jnp.where(
        lane < slots, 1.0 - inside, jnp.where(lane == slots, used, jnp.where(ones, 1.0, 0.0))
    )


def forward_kernel(
    me, tok_other, tok_own, weight, bias_col, start_col, end_col, start_row, end_row,
    att_other, att_own, log_out, qt_out, kaug_out, tokens, qhl, vt, segq,
):
    half = tok_other.shape[0]
    count = 2 * half
    heads = weight.shape[2] // HD
    width = heads * HD
    slots = start_col.shape[0]
    tokens[0:half] = tok_other[...]
    tokens[half:count] = tok_own[...]
    bases = ((1 - me[0]) * half, me[0] * half)
    for part in range(2):
        segq[0 : slots + 1, part * half : (part + 1) * half] = query_rows(
            start_col[...], end_col[...], bases[part], half
        ).astype(bf16)
    segq[slots + 1 :, :] = jnp.zeros((128 - slots - 1, count), bf16)

    step = 512

    def project(i, carry):
        at = pl.multiple_of(i * step, step)
        rows = tokens[pl.ds(at, step), :]
        query = (dot(weight[0], rows, 0, 1) + bias_col[0]).astype(bf16)
        qt_out[:, pl.ds(at, step)] = query
        scaled = query.astype(f32) * (math.log2(math.e) / math.sqrt(HD))
        high = scaled.astype(bf16)
        low = (scaled - high.astype(f32)).astype(bf16)
        value = (dot(weight[2], rows, 0, 1) + bias_col[1]).astype(bf16)
        key = dot(rows, weight[1]).astype(bf16).astype(f32)
        base = jnp.where(at < half, bases[0], bases[1] - half) + at
        common = key_columns(start_row[...], end_row[...], base, step, slots).astype(bf16)
        lane = lax.broadcasted_iota(jnp.int32, (step, 128), 1)
        for h in range(heads):
            qhl[h * 128 : h * 128 + HD, pl.ds(at, step)] = high[h * HD : (h + 1) * HD]
            qhl[h * 128 + HD : (h + 1) * 128, pl.ds(at, step)] = low[h * HD : (h + 1) * HD]
            vt[h * 80 : h * 80 + HD, pl.ds(at, step)] = value[h * HD : (h + 1) * HD]
            vt[h * 80 + HD : (h + 1) * 80, pl.ds(at, step)] = jnp.ones((16, step), bf16)
            if h % 2 == 0:
                pair = key[:, h * HD : h * HD + 128]
                turned = pltpu.roll(pair, HD, 1)
                twice = (jnp.where(lane < HD, pair, turned), jnp.where(lane < HD, turned, pair))
            kaug_out[h, pl.ds(at, step), 0:128] = twice[h % 2].astype(bf16)
            kaug_out[h, pl.ds(at, step), 128:256] = common
        return carry

    lax.fori_loop(0, count // step, project, 0)

    def block(at, out, place):
        seg = segq[:, pl.ds(at, QB)]
        for h in range(heads):
            query = jnp.concatenate([qhl[h * 128 : (h + 1) * 128, pl.ds(at, QB)], seg], axis=0)
            scores = dot(kaug_out[h], query)
            peak = jnp.max(scores, axis=0, keepdims=True)
            probs = jnp.exp2(scores - peak).astype(bf16)
            summed = dot(vt[h * 80 : (h + 1) * 80, :], probs)
            total = summed[HD : HD + 1]
            out[h * HD : (h + 1) * HD, pl.ds(place, QB)] = summed[:HD] / total
            log_out[h : h + 1, pl.ds(at, QB)] = peak + jnp.log2(total)

    for part, out in enumerate((att_other, att_own)):

        def body(i, carry, part=part, out=out):
            place = pl.multiple_of(i * QB, QB)
            block(place + part * half, out, place)
            return carry

        lax.fori_loop(0, half // QB, body, 0)


def attend_forward(me, tokens, weight, bias_col, start_col, end_col, start_row, end_row):
    count, width = tokens.shape[0], weight.shape[2]
    half, heads, depth = count // 2, width // HD, tokens.shape[1]
    whole = lambda a: pl.BlockSpec(a.shape, lambda i, me, n=a.ndim: (0,) * n)
    outs = [
        shape((width, half)),
        shape((width, half)),
        shape((8, count)),
        shape((width, count), bf16),
        shape((heads, count, 256), bf16),
    ]
    return call(
        forward_kernel,
        outs,
        grid_spec=pltpu.PrefetchScalarGridSpec(
            num_scalar_prefetch=1,
            grid=(1,),
            in_specs=[
                pl.BlockSpec((half, depth), lambda i, me: (1 - me[0], 0)),
                pl.BlockSpec((half, depth), lambda i, me: (me[0], 0)),
                *[whole(a) for a in (weight, bias_col, start_col, end_col, start_row, end_row)],
            ],
            out_specs=[whole(o) for o in outs],
            scratch_shapes=[
                pltpu.VMEM((count, depth), bf16),
                pltpu.VMEM((heads * 128, count), bf16),
                pltpu.VMEM((heads * 80, count), bf16),
                pltpu.VMEM((128, count), bf16),
            ],
        ),
    )(me, tokens, tokens, weight, bias_col, start_col, end_col, start_row, end_row)


def norm(v):
    center = v - jnp.mean(v, axis=-1, keepdims=True)
    rstd = lax.rsqrt(jnp.mean(center * center, axis=-1, keepdims=True) + EPS)
    return center * rstd, rstd


def norm_back(grad, n, rstd):
    first = jnp.mean(grad, axis=-1, keepdims=True)
    second = jnp.mean(grad * n, axis=-1, keepdims=True)
    return rstd * (grad - first - n * second)


def normal_parts(h):
    size = jnp.abs(h)
    t = 1.0 / (1.0 + (0.3275911 * math.sqrt(0.5)) * size)
    bell = jnp.exp2(h * h * (-0.5 * math.log2(math.e)))
    poly = t * (
        0.127414796 + t * (-0.142248368 + t * (0.7107068705 + t * (-0.7265760135 + t * 0.5307027145)))
    )
    tail = poly * bell
    below = jnp.where(h < 0, tail, 1.0 - tail)
    return below, bell * (1.0 / math.sqrt(2.0 * math.pi))


def middle_kernel(
    me, att_own, att_rcv, wo_own, wo_rcv, we_own, we_rcv, wr_own, wr_rcv, eb_own, eb_rcv,
    tok, cot, rows, start_row, end_row,
    layer_out, resid_out, ga_own, ga_other, act_out, gh_out, nl_out, gr_out, gb_out, att_out, small, eb_out,
    wo, we, wr,
):
    i = pl.program_id(0)
    units = we_own.shape[1]
    width = wo_own.shape[0]
    count = tok.shape[0]

    @pl.when(i == 0)
    def _():
        wo[0:width] = wo_own[...]
        wo[width:] = wo_rcv[...].astype(bf16)
        we[:, 0:units] = we_own[...]
        we[:, units:] = we_rcv[...].astype(bf16)
        wr[0:units] = wr_own[...]
        wr[units:] = wr_rcv[...].astype(bf16)
        small[...] = jnp.zeros_like(small)
        eb_out[...] = jnp.zeros_like(eb_out)

    output_bias, gain1, shift1, reduce_bias, gain2, shift2 = (rows[j : j + 1] for j in range(6))
    base = (me[0] * pl.num_programs(0) + i) * count
    place = lax.broadcasted_iota(jnp.int32, (count, 128), 0) + base
    inside = jnp.where((place >= start_row[...]) & (place < end_row[...]), 1.0, 0.0)
    valid = jnp.sum(inside, axis=1, keepdims=True)

    att = jnp.concatenate([att_own[...], att_rcv[...]], axis=0).astype(bf16)
    att_out[...] = att
    resid_one = tok[...].astype(f32) + (dot(att, wo[...], 0, 0) + output_bias)
    n1, rstd1 = norm(resid_one)
    normed = n1 * gain1 + shift1
    normed_low = normed.astype(bf16)
    nl_out[...] = normed_low
    bias = jnp.concatenate([eb_own[...], eb_rcv[...]], axis=1)
    hidden = dot(normed_low, we[...]) + bias
    below, density = normal_parts(hidden)
    active = (hidden * below).astype(bf16)
    slope = below + hidden * density
    act_out[...] = active
    resid_two = normed + (dot(active, wr[...]) + reduce_bias)
    n2, rstd2 = norm(resid_two)
    layer_out[...] = ((n2 * gain2 + shift2) * valid).astype(bf16).astype(f32)
    grad = cot[...].astype(f32) * valid
    column = lambda v: jnp.sum(v, axis=0, keepdims=True)
    small[0:1] += column(grad * n2)
    small[1:2] += column(grad)
    grad_two = norm_back(grad * gain2, n2, rstd2)
    grad_result = grad_two.astype(bf16)
    gr_out[...] = grad_result
    small[2:3] += column(grad_result.astype(f32))
    grad_hidden = (dot(grad_result, wr[...], 1, 1) * slope).astype(bf16)
    gh_out[...] = grad_hidden
    eb_out[0:1] += column(grad_hidden.astype(f32))
    grad_normed = grad_two + dot(grad_hidden, we[...], 1, 1)
    small[3:4] += column(grad_normed * n1)
    small[4:5] += column(grad_normed)
    grad_one = norm_back(grad_normed * gain1, n1, rstd1)
    resid_out[...] = grad_one
    grad_branch = grad_one.astype(bf16)
    gb_out[...] = grad_branch
    small[5:6] += column(grad_branch.astype(f32))
    grad_att = dot(wo[...], grad_branch, 1, 1).astype(bf16).astype(f32)
    ga_own[...] = grad_att[0:width]
    ga_other[...] = grad_att[width:]


def middle(me, att_own, att_rcv, wo_own, wo_rcv, we_own, we_rcv, wr_own, wr_rcv, eb_own, eb_rcv, tokens, cotangent, rows, start_row, end_row):
    half, depth = tokens.shape[0] // 2, tokens.shape[1]
    width, units = wo_own.shape[0], we_own.shape[1]
    blk = 256
    steps = half // blk
    whole = lambda a: pl.BlockSpec(a.shape, lambda i, me, n=a.ndim: (0,) * n)
    by_row = lambda n: pl.BlockSpec((blk, n), lambda i, me: (i, 0))
    by_col = lambda n: pl.BlockSpec((n, blk), lambda i, me: (0, i))
    mine = pl.BlockSpec((blk, depth), lambda i, me: (me[0] * steps + i, 0))
    outs = [
        (shape((half, depth)), by_row(depth)),
        (shape((half, depth)), by_row(depth)),
        (shape((width, half)), by_col(width)),
        (shape((width, half)), by_col(width)),
        (shape((half, 2 * units), bf16), by_row(2 * units)),
        (shape((half, 2 * units), bf16), by_row(2 * units)),
        (shape((half, depth), bf16), by_row(depth)),
        (shape((half, depth), bf16), by_row(depth)),
        (shape((half, depth), bf16), by_row(depth)),
        (shape((2 * width, half), bf16), by_col(2 * width)),
        (shape((8, depth)), None),
        (shape((8, 2 * units)), None),
    ]
    args = (wo_own, wo_rcv, we_own, we_rcv, wr_own, wr_rcv, eb_own, eb_rcv)
    return call(
        middle_kernel,
        [o for o, _ in outs],
        grid_spec=pltpu.PrefetchScalarGridSpec(
            num_scalar_prefetch=1,
            grid=(steps,),
            in_specs=[
                by_col(width),
                by_col(width),
                *[whole(a) for a in args],
                mine,
                mine,
                *[whole(a) for a in (rows, start_row, end_row)],
            ],
            out_specs=[s or whole(o) for o, s in outs],
            scratch_shapes=[
                pltpu.VMEM((2 * width, depth), bf16),
                pltpu.VMEM((depth, 2 * units), bf16),
                pltpu.VMEM((2 * units, depth), bf16),
            ],
        ),
    )(me, att_own, att_rcv, *args, tokens, cotangent, rows, start_row, end_row)


def reduce_grad_kernel(act, gr, out):
    out[...] = dot(act[...], gr[...], 0, 0)


def expand_grad_kernel(nl, gh, out):
    out[...] = dot(nl[...], gh[...], 0, 0)


def reduce_grad(active, grad_result, which):
    half, units, depth = active.shape[0], active.shape[1] // 2, grad_result.shape[1]
    steps = 4
    blk = units // steps
    return call(
        reduce_grad_kernel,
        shape((units, depth)),
        grid=(steps,),
        in_specs=[
            pl.BlockSpec((half, blk), lambda i: (0, which * steps + i)),
            pl.BlockSpec((half, depth), lambda i: (0, 0)),
        ],
        out_specs=pl.BlockSpec((blk, depth), lambda i: (i, 0)),
    )(active, grad_result)


def expand_grad(normed_low, grad_hidden, which):
    half, units, depth = grad_hidden.shape[0], grad_hidden.shape[1] // 2, normed_low.shape[1]
    steps = 4
    blk = units // steps
    return call(
        expand_grad_kernel,
        shape((depth, units)),
        grid=(steps,),
        in_specs=[
            pl.BlockSpec((half, depth), lambda i: (0, 0)),
            pl.BlockSpec((half, blk), lambda i: (0, which * steps + i)),
        ],
        out_specs=pl.BlockSpec((depth, blk), lambda i: (0, i)),
    )(normed_low, grad_hidden)


def output_grad_kernel(att, gb, own, other):
    width = own.shape[0]
    both = dot(att[...], gb[...])
    own[...] = both[:width]
    other[...] = both[width:]


def output_grad(att, grad_branch):
    width, depth = att.shape[0] // 2, grad_branch.shape[1]
    return call(output_grad_kernel, [shape((width, depth)), shape((width, depth))])(att, grad_branch)


def backward_kernel(
    me, tok_other, tok_own, weight, bias_row, start_col, end_col, qt, kaug, logs, att_other, att_own,
    ga_other, ga_own, dq, dk, dv, kt, vaug, segq, dkt, dvt,
):
    head = pl.program_id(0)
    half = tok_other.shape[0]
    count = 2 * half
    heads = weight.shape[2] // HD
    slots = start_col.shape[0]
    scale = HD**-0.5

    @pl.when(head == 0)
    def _():
        bases = ((1 - me[0]) * half, me[0] * half)
        for part, tok in enumerate((tok_other, tok_own)):
            segq[0 : slots + 1, part * half : (part + 1) * half] = query_rows(
                start_col[...], end_col[...], bases[part], half
            ).astype(bf16)
            kt[:, part * half : (part + 1) * half] = dot(weight[1], tok[...], 0, 1).astype(bf16)
            value = (dot(tok[...], weight[2]) + bias_row[...]).astype(bf16).astype(f32)
            lane = lax.broadcasted_iota(jnp.int32, (half, 128), 1)
            ones = jnp.where(lane < HD + 3, 1.0, 0.0)
            for h in range(heads):
                pair = value[:, h // 2 * 128 : h // 2 * 128 + 128]
                if h % 2:
                    pair = pltpu.roll(pair, HD, 1)
                vaug[h, part * half : (part + 1) * half, :] = jnp.where(
                    lane < HD, pair, ones
                ).astype(bf16)

    dkt[...] = jnp.zeros_like(dkt)
    dvt[...] = jnp.zeros_like(dvt)
    zeros_q = jnp.zeros((128 - slots - 4, QB), bf16)
    zeros_v = jnp.zeros((128 - HD - 3, QB), bf16)

    for part, (att, ga) in enumerate(((att_other, ga_other), (att_own, ga_own))):

        def body(i, carry, part=part, att=att, ga=ga):
            place = pl.multiple_of(i * QB, QB)
            at = place + part * half
            grad = ga[:, pl.ds(place, QB)]
            inner = -jnp.sum(grad * att[:, pl.ds(place, QB)], axis=0, keepdims=True)
            grad_low = grad.astype(bf16)
            upper = jnp.concatenate([grad_low, *split3(inner), zeros_v], axis=0)
            query = qt[:, pl.ds(at, QB)]
            scaled = query.astype(f32) * (math.log2(math.e) / math.sqrt(HD))
            high = scaled.astype(bf16)
            low = (scaled - high.astype(f32)).astype(bf16)
            logs_q = logs[pl.ds(head, 1), pl.ds(at, QB)]
            seg = segq[0 : slots + 1, pl.ds(at, QB)]
            left = jnp.concatenate([high, low, seg, *split3(-logs_q), zeros_q], axis=0)
            probs = jnp.exp2(dot(kaug[0], left))
            grad_probs = dot(vaug[head], upper)
            grad_scores = (probs * grad_probs).astype(bf16)
            dvt[...] += dot(grad_low, probs.astype(bf16), 1, 1)
            dkt[...] += dot(query, grad_scores, 1, 1)
            dq[:, pl.ds(at, QB)] = (
                dot(kt[pl.ds(pl.multiple_of(head * HD, HD), HD), :], grad_scores) * scale
            ).astype(bf16)
            return carry

        lax.fori_loop(0, half // QB, body, 0)
    dk[...] = (dkt[...] * scale).astype(bf16)
    dv[...] = dvt[...].astype(bf16)


def attend_backward(me, tokens, weight, bias_row, start_col, end_col, qt, kaug, logs, att_other, att_own, ga_other, ga_own):
    count, width = tokens.shape[0], weight.shape[2]
    half, heads, depth = count // 2, width // HD, tokens.shape[1]
    slots = start_col.shape[0]
    whole = lambda a: pl.BlockSpec(a.shape, lambda i, me, n=a.ndim: (0,) * n)
    by_head = lambda n: pl.BlockSpec((HD, n), lambda i, me: (i, 0))
    outs = [shape((width, count), bf16)] * 3
    return call(
        backward_kernel,
        outs,
        grid_spec=pltpu.PrefetchScalarGridSpec(
            num_scalar_prefetch=1,
            grid=(heads,),
            in_specs=[
                pl.BlockSpec((half, depth), lambda i, me: (1 - me[0], 0)),
                pl.BlockSpec((half, depth), lambda i, me: (me[0], 0)),
                *[whole(a) for a in (weight, bias_row, start_col, end_col)],
                by_head(count),
                pl.BlockSpec((1, count, 256), lambda i, me: (i, 0, 0)),
                whole(logs),
                *[by_head(half)] * 4,
            ],
            out_specs=[by_head(count)] * 3,
            scratch_shapes=[
                pltpu.VMEM((width, count), bf16),
                pltpu.VMEM((heads, count, 128), bf16),
                pltpu.VMEM((slots + 1, count), bf16),
                pltpu.VMEM((HD, count), f32),
                pltpu.VMEM((HD, count), f32),
            ],
        ),
    )(me, tokens, tokens, weight, bias_row, start_col, end_col, qt, kaug, logs, att_other, att_own, ga_other, ga_own)


def project_back_kernel(me, tok_other, tok_own, weight, dq, dk, dv, grad, bias, rows_other, rows_own):
    half = tok_other.shape[0]
    for c, part in enumerate((dq, dk, dv)):
        turned = dot(part[:, 0:half], tok_other[...]) + dot(part[:, half:], tok_own[...])
        grad[c] = turned.T
        if c != 1:
            bias[:, c // 2 : c // 2 + 1] = jnp.sum(part[...].astype(f32), axis=1, keepdims=True)
    for at, out in ((0, rows_other), (half, rows_own)):
        out[...] = sum(
            dot(part[:, at : at + half], weight[c], 0, 1) for c, part in enumerate((dq, dk, dv))
        )


def project_back(me, tokens, weight, dq, dk, dv):
    half, depth, width = tokens.shape[0] // 2, tokens.shape[1], weight.shape[2]
    whole = lambda a: pl.BlockSpec(a.shape, lambda i, me, n=a.ndim: (0,) * n)
    outs = [shape((3, depth, width)), shape((width, 2)), shape((half, depth)), shape((half, depth))]
    return call(
        project_back_kernel,
        outs,
        grid_spec=pltpu.PrefetchScalarGridSpec(
            num_scalar_prefetch=1,
            grid=(1,),
            in_specs=[
                pl.BlockSpec((half, depth), lambda i, me: (1 - me[0], 0)),
                pl.BlockSpec((half, depth), lambda i, me: (me[0], 0)),
                *[whole(a) for a in (weight, dq, dk, dv)],
            ],
            out_specs=[whole(o) for o in outs],
        ),
    )(me, tokens, tokens, weight, dq, dk, dv)


def add_rows_kernel(a, b, c, out):
    out[...] = (a[...] + b[...] + c[...]).astype(bf16).astype(f32)


def add_rows(a, b, c):
    rows, depth = a.shape
    blk = pl.BlockSpec((rows // 4, depth), lambda i: (i, 0))
    return call(add_rows_kernel, shape(a.shape), grid=(4,), in_specs=[blk] * 3, out_specs=blk)(a, b, c)


def join_kernel(me, own, other, out):
    mine = pl.program_id(0) == me[0]

    @pl.when(mine)
    def _():
        out[...] = own[...].astype(bf16)

    @pl.when(jnp.logical_not(mine))
    def _():
        out[...] = other[...].astype(bf16)


def join(me, own, other):
    half, depth = own.shape
    whole = pl.BlockSpec((half, depth), lambda i, me: (0, 0))
    return call(
        join_kernel,
        shape((2 * half, depth), bf16),
        grid_spec=pltpu.PrefetchScalarGridSpec(
            num_scalar_prefetch=1,
            grid=(2,),
            in_specs=[whole, whole],
            out_specs=pl.BlockSpec((half, depth), lambda i, me: (i, 0)),
        ),
    )(me, own, other)


def swap(v):
    return lax.ppermute(v, "mp", [(0, 1), (1, 0)])


def local(
    tokens, seq_starts, seq_lengths, attend_weight, attend_bias, output_weight, output_bias, first_gain, first_shift,
    expand_weight, expand_bias, reduce_weight, reduce_bias, second_gain, second_shift, cotangent,
):
    slots = seq_starts.shape[1]
    me = lax.axis_index("mp").astype(jnp.int32)[None]
    ends = seq_starts + seq_lengths
    start_col, end_col = seq_starts.reshape(slots, 1), ends.reshape(slots, 1)
    start_row = jnp.pad(seq_starts, ((0, 0), (0, 128 - slots)))
    end_row = jnp.pad(ends, ((0, 0), (0, 128 - slots)))
    bias_col = attend_bias[:, :, None]
    eb_own = expand_bias[None, :]
    wide = widen(output_weight, expand_weight, reduce_weight)
    wo_rcv, we_rcv, wr_rcv = (swap(w) for w in wide)
    eb_rcv = swap(eb_own)

    att_other, att_own, logs, qt, kaug = attend_forward(
        me, tokens, attend_weight, bias_col, start_col, end_col, start_row, end_row
    )
    att_rcv = swap(att_other)
    rows = jnp.stack(
        [output_bias, first_gain, first_shift, reduce_bias, second_gain, second_shift, first_gain, first_gain]
    )
    (layer_own, resid, ga_own, ga_other, active, gh, nl, gr, gb, att, small, eb_grad) = middle(
        me, att_own, att_rcv, output_weight, wo_rcv, expand_weight, we_rcv, reduce_weight, wr_rcv,
        eb_own, eb_rcv, tokens, cotangent, rows, start_row, end_row,
    )
    ga_rcv = swap(ga_other)
    layer_rcv = swap(layer_own)
    grad_reduce = reduce_grad(active, gr, 0) + swap(reduce_grad(active, gr, 1))
    grad_expand = expand_grad(nl, gh, 0) + swap(expand_grad(nl, gh, 1))
    out_own, out_other = output_grad(att, gb)
    grad_output = out_own + swap(out_other)
    units = expand_weight.shape[1]
    eb_sum = eb_grad[0, :units] + swap(eb_grad[0, units:])

    dq, dk, dv = attend_backward(
        me, tokens, attend_weight, attend_bias[1:2], start_col, end_col, qt, kaug, logs,
        att_other, att_own, ga_rcv, ga_own,
    )
    grad_attend, bias_grad, rows_other, rows_own = project_back(me, tokens, attend_weight, dq, dk, dv)
    mine = add_rows(rows_own, swap(rows_other), resid)
    grad_tokens = join(me, mine, swap(mine))
    layer_out = join(me, layer_own, layer_rcv)

    small = lax.psum(small, ("dp", "mp"))
    grad_attbias, grad_expbias = lax.psum((bias_grad.T, eb_sum), "dp")
    grad_attend, grad_output, grad_expand, grad_reduce = lax.psum(
        (grad_attend, grad_output, grad_expand, grad_reduce), "dp"
    )
    return (
        layer_out,
        grad_tokens,
        grad_attend,
        grad_attbias,
        grad_output,
        small[5],
        small[3],
        small[4],
        grad_expand,
        grad_expbias,
        grad_reduce,
        small[2],
        small[0],
        small[1],
    )


def solution(mesh):
    return jax.shard_map(
        local,
        mesh=mesh,
        in_specs=(
            P("dp", None),
            P("dp", None),
            P("dp", None),
            P(None, None, "mp"),
            P(None, "mp"),
            P("mp", None),
            P(),
            P(),
            P(),
            P(None, "mp"),
            P("mp"),
            P("mp", None),
            P(),
            P(),
            P(),
            P("dp", None),
        ),
        out_specs=(
            P("dp", None),
            P("dp", None),
            P(None, None, "mp"),
            P(None, "mp"),
            P("mp", None),
            P(),
            P(),
            P(),
            P(None, "mp"),
            P("mp"),
            P("mp", None),
            P(),
            P(),
            P(),
        ),
        check_vma=False,
    )
```

time: 748 us -> 421 us (0.56); the launches traced: 739 us -> 420 us
  matrix products: 242 us -> 0 us
  Pallas kernels: 0 us -> 173 us
  waiting for transfers between devices: 224 us -> 82 us
  other arithmetic: 104 us -> 7.83 us
  local copies, waits for them, and re-layouts: 59.6 us -> 17.6 us
  blocking collectives: 80.3 us -> 122 us
  starting transfers between devices: 13.1 us -> 3.79 us
    dot_general x40 -> x0, matrix products: 242 us -> none  [the longest x4 45.2 us: backward_block(): jnp.einsum('qhd,khd->hqk', grad_blk, value_all, preferred_element_type=f32)]
    pallas_call x0 -> x13, Pallas kernels: none -> 173 us  [the longest x1 52.2 us: attend_backward(): call(backward_kernel, outs, grid_spec=pltpu.PrefetchScalarGridSpec(num_sc...]
    psum x5 -> x1, waiting for transfers between devices: 224 us -> 77.1 us  [local(): lax.psum((grad_attend, grad_output, grad_expand, grad_reduce), 'dp')]
    convert_element_type x6 -> x0, other arithmetic: 48.8 us -> none  [the longest x4 43.6 us: backward_block(): grad_scores = (probs * (grad_probs - inner)).astype(bf16)]
    reduce_sum x17 -> x0, other arithmetic: 45.4 us -> none  [the longest x4 17.3 us: forward_block(): total = jnp.sum(jnp.exp(scores - peak), axis=-1, keepdims=True)]
    psum x1 -> x2, blocking collectives: 80.3 us -> 122 us  [the longest x1 77.1 us: local(): grad_attbias, grad_expbias = lax.psum((bias_grad.T, eb_sum), 'dp')]
    unnamed x106 -> x53, local copies, waits for them, and re-layouts: 27.1 us -> 11.8 us
    another operation x9 -> x1, local copies, waits for them, and re-layouts: 14.8 us -> 0.64 us  [local(): jnp.stack([output_bias, first_gain, first_shift, reduce_bias, second_gain...]
  transfers between devices with their start and end apart: 5 -> 14, of which waited for: 4 -> 4; matrix products, arithmetic and copies ran while one was open for 3% -> 3% of each run, Pallas kernels for 0% -> 33%
where the time goes in v1:
time: 421 us; the launch traced here: 420 us
  Pallas kernels  173 us (41%)
  blocking collectives  122 us (29%)
  waiting for transfers between devices  82 us (19%)
  local copies, waits for them, and re-layouts  17.6 us (4%)
  between operations  14.2 us (3%)
  other arithmetic  7.83 us (2%)
    psum x1, waiting for transfers between devices, local(): lax.psum((grad_attend, grad_output, grad_expand, grad_reduce), 'dp')  77.1 us
    psum x1, blocking collectives, local(): grad_attbias, grad_expbias = lax.psum((bias_grad.T, eb_sum), 'dp')  77.1 us
    pallas_call x1, Pallas kernels, attend_backward(): call(backward_kernel, outs, grid_spec=pltpu.PrefetchScalarGridSpec(num_sc...  52.2 us
    pallas_call x1, Pallas kernels, attend_forward(): call(forward_kernel, outs, grid_spec=pltpu.PrefetchScalarGridSpec(num_sca...  46.6 us
    psum x1, blocking collectives, local(): small = lax.psum(small, ('dp', 'mp'))  44.7 us
    pallas_call x1, Pallas kernels, middle(): call(middle_kernel, [o for o, _ in outs], grid_spec=pltpu.PrefetchScalarG...  26 us
    unnamed x53, local copies, waits for them, and re-layouts  11.8 us
    pallas_call x2, Pallas kernels, expand_grad(): call(expand_grad_kernel, shape((depth, units)), grid=(steps,), in_specs=[...  10.4 us
  transfers between devices with their start and end apart: 14, of which 4 were waited for; matrix products, arithmetic and copies ran while one was open for 3% of the time, Pallas kernels for 33%

profile of v1, /device:TPU:0, one launch (start us, length us, event | category | flops | bytes accessed | tf_op | source)
XLA Modules:
  0.0 420.4 jit_solution(12457618113773508047)
XLA Ops:
  7.3 3.9 shard_map.264
  11.2 0.5 collective-permute-start.2
  11.7 0.5 pad.7.start_row
  12.2 0.5 pad.8.end_row
  12.7 0.7 copy.37.end_col
  13.4 0.7 copy.36.start_col
  14.1 0.9 copy.35.bias_col
  15.0 46.6 %shard_map.263 = (f32[256,1024]{1,0:T(8,128)}, f32[256,1024]{1,0:T(8,128)}, f32[8,2048]{1,0:T(8,128)}, bf16[256,2048]{1,0:T(8,128)(2,1)}, bf16[4,2048,256]{2,1,0:T(8,128)(2,1)}) custom-call(s32[1]{0:T(128)} %bitcast.me, bf16[2048,512]{1,0:T(8,128)(2,1)} %tok_own.5, bf16[2048,512]{1,0:T(8,128)(2,1)} %tok_own.5, bf16[3,512,256]{2,1,0:T(8,128)(2,1)} %weight.5, ...), custom_call_target="tpu_custom_call" | custom-call | tf_op jit(solution)/shard_map/pallas_call | solution.py:159
  61.6 0.4 collective-permute-start
  62.2 0.4 collective-permute-start.4
  62.6 0.6 stack.29.rows
  63.3 1.8 collective-permute-done.4.eb_rcv
  65.1 0.3 collective-permute-done.1.wo_rcv
  65.7 0.8 copy-done.6
  66.5 0.7 copy-done.3
  67.1 26.0 %shard_map.265 = (f32[1024,512]{1,0:T(8,128)}, f32[1024,512]{1,0:T(8,128)}, f32[256,1024]{1,0:T(8,128)}, f32[256,1024]{1,0:T(8,128)}, bf16[1024,2048]{1,0:T(8,12...) custom-call(s32[1]{0:T(128)} %bitcast.me, ...), custom_call_target="tpu_custom_call" | custom-call | tf_op jit(solution)/shard_map/pallas_call | solution.py:297
  93.2 5.0 %shard_map.275 = f32[1024,512]{1,0:T(8,128)} custom-call(bf16[1024,2048]{1,0:T(8,128)(2,1)} %get-tuple-element.70.act, bf16[1024,512]{1,0:T(8,128)(2,1)} %get-tuple-element.71.gr), custom_call_target="tpu_custom_call" | custom-call | tf_op jit(solution)/shard_map/pallas_call | solution.py:333
  98.2 0.3 collective-permute-start.12
  98.6 5.2 %shard_map.273 = f32[512,1024]{1,0:T(8,128)} custom-call(bf16[1024,512]{1,0:T(8,128)(2,1)} %get-tuple-element.67.nl, bf16[1024,2048]{1,0:T(8,128)(2,1)} %get-tuple-element.68.gh), custom_call_target="tpu_custom_call" | custom-call | tf_op jit(solution)/shard_map/pallas_call | solution.py:349
  104.3 3.1 shard_map.271
  107.6 0.6 slice.27.bias_row
  108.2 5.0 %shard_map.274 = f32[1024,512]{1,0:T(8,128)} custom-call(bf16[1024,2048]{1,0:T(8,128)(2,1)} %get-tuple-element.70.act, bf16[1024,512]{1,0:T(8,128)(2,1)} %get-tuple-element.71.gr), custom_call_target="tpu_custom_call" | custom-call | tf_op jit(solution)/shard_map/pallas_call | solution.py:333
  113.2 5.2 %shard_map.272 = f32[512,1024]{1,0:T(8,128)} custom-call(bf16[1024,512]{1,0:T(8,128)(2,1)} %get-tuple-element.67.nl, bf16[1024,2048]{1,0:T(8,128)(2,1)} %get-tuple-element.68.gh), custom_call_target="tpu_custom_call" | custom-call | tf_op jit(solution)/shard_map/pallas_call | solution.py:349
  118.4 0.9 add.34
  119.3 1.0 copy-done.7
  120.2 52.2 %shard_map.267 = (bf16[256,2048]{1,0:T(8,128)(2,1)}, bf16[256,2048]{1,0:T(8,128)(2,1)}, bf16[256,2048]{1,0:T(8,128)(2,1)}) custom-call(s32[1]{0:T(128)} %bitcast.me, bf16[2048,512]{1,0:T(8,128)(2,1)} %tok_own.5, bf16[2048,512]{1,0:T(8,128)(2,1)} %tok_own.5, bf16[3,512,256]{2,1,0:T(8,128)(2,1)} %weight.5, f32[1,256]{1,0:T(1,128)} %slice.27.bias_row, ...), custom_call_target="tpu_custom_call" | custom-call | tf_op jit(solution)/shard_map/pallas_call | solution.py:446
  172.5 8.2 %shard_map.268 = (f32[3,512,256]{2,1,0:T(8,128)}, f32[256,2]{1,0:T(8,128)}, f32[1024,512]{1,0:T(8,128)}, f32[1024,512]{1,0:T(8,128)}) custom-call(s32[1]{0:T(128)} %bitcast.me, bf16[2048,512]{1,0:T(8,128)(2,1)} %tok_own.5, bf16[2048,512]{1,0:T(8,128)(2,1)} %tok_own.5, bf16[3,512,256]{2,1,0:T(8,128)(2,1)} %weight.5, bf16[256,2048]{1,0:T(8,128)(2,1)} %get-tuple-element.54.dq, ...), custom_call_target="tpu_custom_call" | custom-call | tf_op jit(solution)/shard_map/pallas_call | solution.py:490
  180.7 3.6 add.37
  184.3 3.3 add.35
  187.7 0.4 collective-permute-start.7
  188.1 1.1 copy-done.2
  189.3 0.3 collective-permute-start.5
  189.6 2.7 collective-permute-done.7.b
  192.3 4.8 %shard_map.269.own = f32[1024,512]{1,0:T(8,128)} custom-call(f32[1024,512]{1,0:T(8,128)} %get-tuple-element.57.a, f32[1024,512]{1,0:T(8,128)} %collective-permute-done.7.b, f32[1024,512]{1,0:T(8,128)} %get-tuple-element.59.c), custom_call_target="tpu_custom_call" | custom-call | tf_op jit(solution)/shard_map/pallas_call | solution.py:513
  197.1 0.4 collective-permute-start.8
  197.4 0.8 fusion
  198.3 44.7 %psum.52 = f32[8,512]{1,0:T(8,128)S(1)} all-reduce(f32[8,512]{1,0:T(8,128)S(1)} %copy-done.12), channel_id=1, replica_groups=mesh['dp'=16,'mp'=2] {'dp','mp'}, use_global_device_ids=true, to_apply=%region_3.4 | all-reduce | flops 4096 | bytes 32768 | tf_op jit(solution)/shard_map/psum | solution.py:592
  243.1 0.6 fusion.1
  243.7 77.1 %all-reduce.2 = (f32[2,256]{0,1:T(8,128)S(1)}, f32[1024]{0:T(1024)}) all-reduce(f32[2,256]{0,1:T(8,128)S(1)} %bitcast.20, f32[1024]{0:T(1024)S(1)} %add.36), channel_id=1, replica_groups=mesh['dp'=16,'mp'=2] {'dp'}, use_global_device_ids=true, to_apply=%region_1.2 | all-reduce | flops 1536 | bytes 12288 | tf_op jit(solution)/shard_map/psum | solution.py:593
  320.8 0.7 copy.40
  321.4 3.7 shard_map.266
  325.2 3.9 shard_map.270
  329.1 77.1 %all-reduce.6.cloned.1.call-done = (f32[3,512,256]{2,1,0:T(8,128)}, f32[256,512]{1,0:T(8,128)}, f32[512,1024]{1,0:T(8,128)}, f32[1024,512]{1,0:T(8,128)}) async-done(((f32[3,512,256]{2,1,0:T(8,128)}, f32[256,512]{1,0:T(8,128)}, f32[512,1024]{1,0:T(8,128)}, f32[1024,512]{1,0:T(8,128)}), (f32[3,512,256]{2,1,0:T(8,128)}, f32[256,512]{1,0:T(8,128)}, f32[512,1024]{1,0:T(8,128)}, ...) | async-done | bytes 6291472 | tf_op jit(solution)/shard_map/psum | solution.py:594
  406.2 2.8 copy.45
  409.0 0.8 copy.46
  409.8 1.3 copy.47
  411.2 1.0 copy-done.4
  412.2 1.3 copy.48
  (63 shorter events, 1.3 us)
Async XLA Ops:
  7.2 4.5 %copy-start.21 = (s32[1,16]{1,0:T(1,128)S(1)}, s32[1,16]{1,0:T(1,128)}, u32[]{:S(2)}) copy-start(s32[1,16]{1,0:T(1,128)} %param.17) | copy-start | bytes 196
  7.2 4.5 %copy-start.23 = (s32[1,16]{1,0:T(1,128)S(1)}, s32[1,16]{1,0:T(1,128)}, u32[]{:S(2)}) copy-start(s32[1,16]{1,0:T(1,128)} %param.18) | copy-start | bytes 196
  7.2 6.9 %copy-start.13 = (f32[2,256]{1,0:T(2,128)S(1)}, f32[2,256]{1,0:T(2,128)}, u32[]{:S(2)}) copy-start(f32[2,256]{1,0:T(2,128)} %param.20) | copy-start | bytes 6148
  7.2 399.0 %all-reduce.6.cloned.1.call-start = ((), (), s32[]{:S(2)}) async-start(), calls=%async_computation | async-start | bytes 12582912 | tf_op jit(solution)/shard_map/psum | solution.py:594
  11.2 54.3 %collective-permute-start.2 = (f32[512,1024]{1,0:T(8,128)}, f32[512,1024]{1,0:T(8,128)S(1)}, u32[]{:S(2)}, u32[]{:S(2)}) collective-permute-start(f32[512,1024]{1,0:T(8,128)} %get-tuple-element.46), channel_id=1, source_target_pairs={{0,1},{1,0},{2,3},{3,2},{4,5},{5,4},{6,7},{7,6},{8,9},{9,8},{10,11... | collective-permute-start | bytes 6291464 | tf_op jit(solution)/shard_map/ppermute | solution.py:544
  11.6 53.8 %collective-permute-start.3 = (f32[1024,512]{1,0:T(8,128)}, f32[1024,512]{1,0:T(8,128)}, u32[]{:S(2)}, u32[]{:S(2)}) collective-permute-start(f32[1024,512]{1,0:T(8,128)} %get-tuple-element.47), channel_id=1, source_target_pairs={{0,1},{1,0},{2,3},{3,2},{4,5},{5,4},{6,7},{7,6},{8,9},{9,8},{10,11... | collective-permute-start | bytes 6291464 | tf_op jit(solution)/shard_map/ppermute | solution.py:544
  15.0 47.2 %copy-start.14 = (f32[1024]{0:T(1024)S(1)}, f32[1024]{0:T(1024)}, u32[]{:S(2)}) copy-start(f32[1024]{0:T(1024)} %param.26) | copy-start | bytes 12292
  15.0 47.6 %copy-start.11 = (f32[512]{0:T(512)S(1)}, f32[512]{0:T(512)}, u32[]{:S(2)}) copy-start(f32[512]{0:T(512)} %param.23) | copy-start | bytes 6148
  15.0 47.6 %copy-start.16 = (f32[512]{0:T(512)S(1)}, f32[512]{0:T(512)}, u32[]{:S(2)}) copy-start(f32[512]{0:T(512)} %param.22) | copy-start | bytes 6148
  15.0 47.6 %copy-start.17 = (f32[512]{0:T(512)S(1)}, f32[512]{0:T(512)}, u32[]{:S(2)}) copy-start(f32[512]{0:T(512)} %param.24) | copy-start | bytes 6148
  15.0 47.6 %copy-start.18 = (f32[512]{0:T(512)S(1)}, f32[512]{0:T(512)}, u32[]{:S(2)}) copy-start(f32[512]{0:T(512)} %param.28) | copy-start | bytes 6148
  15.0 47.6 %copy-start.19 = (f32[512]{0:T(512)S(1)}, f32[512]{0:T(512)}, u32[]{:S(2)}) copy-start(f32[512]{0:T(512)} %param.29) | copy-start | bytes 6148
  15.0 47.6 %copy-start.20 = (f32[512]{0:T(512)S(1)}, f32[512]{0:T(512)}, u32[]{:S(2)}) copy-start(f32[512]{0:T(512)} %param.30) | copy-start | bytes 6148
  61.6 3.8 collective-permute-start
  62.1 3.4 collective-permute-start.1
  62.2 3.0 collective-permute-start.4
  65.1 0.6 copy-start.15
  65.5 1.0 copy-start.6
  65.5 1.7 copy-start.3
  98.2 82.5 %collective-permute-start.12 = (f32[1024,512]{1,0:T(8,128)}, f32[1024,512]{1,0:T(8,128)}, u32[]{:S(2)}, u32[]{:S(2)}) collective-permute-start(f32[1024,512]{1,0:T(8,128)} %shard_map.275), channel_id=1, source_target_pairs={{0,1},{1,0},{2,3},{3,2},{4,5},{5,4},{6,7},{7,6},{8,9},{9,8},{10,11... | collective-permute-start | bytes 6291464 | tf_op jit(solution)/shard_map/ppermute | solution.py:544
  98.6 5.4 %copy-start.22 = (f32[256,1024]{1,0:T(8,128)S(1)}, f32[256,1024]{1,0:T(8,128)}, u32[]{:S(2)}) copy-start(f32[256,1024]{1,0:T(8,128)} %get-tuple-element.52) | copy-start | bytes 3145732
  103.8 80.5 %collective-permute-start.10 = (f32[512,1024]{1,0:T(8,128)}, f32[512,1024]{1,0:T(8,128)}, u32[]{:S(2)}, u32[]{:S(2)}) collective-permute-start(f32[512,1024]{1,0:T(8,128)} %shard_map.273), channel_id=1, source_target_pairs={{0,1},{1,0},{2,3},{3,2},{4,5},{5,4},{6,7},{7,6},{8,9},{9,8},{10,11... | collective-permute-start | bytes 6291464 | tf_op jit(solution)/shard_map/ppermute | solution.py:544
  104.0 15.3 %collective-permute-start.6 = (f32[256,1024]{1,0:T(8,128)S(1)}, f32[256,1024]{1,0:T(8,128)S(1)}, u32[]{:S(2)}, u32[]{:S(2)}) collective-permute-start(f32[256,1024]{1,0:T(8,128)S(1)} %copy-done.22), channel_id=1, source_target_pairs={{0,1},{1,0},{2,3},{3,2},{4,5},{5,4},{6,7},{7,6},{8,9},{9,8},{10,11... | collective-permute-start | bytes 3145736 | tf_op jit(solution)/shard_map/ppermute | solution.py:544
  107.4 10.9 %collective-permute-start.9 = (f32[256,512]{1,0:T(8,128)}, f32[256,512]{1,0:T(8,128)S(1)}, u32[]{:S(2)}, u32[]{:S(2)}) collective-permute-start(f32[256,512]{1,0:T(8,128)} %get-tuple-element.65), channel_id=1, source_target_pairs={{0,1},{1,0},{2,3},{3,2},{4,5},{5,4},{6,7},{7,6},{8,9},{9,8},{10,11... | collective-permute-start | bytes 1572872 | tf_op jit(solution)/shard_map/ppermute | solution.py:544
  113.2 5.2 %copy-start.8 = (f32[256,512]{1,0:T(8,128)S(1)}, f32[256,512]{1,0:T(8,128)}, u32[]{:S(2)}) copy-start(f32[256,512]{1,0:T(8,128)} %get-tuple-element.64) | copy-start | bytes 1572868
  119.2 1.0 copy-start.7
  172.5 8.2 %copy-start.1 = (f32[1024,512]{1,0:T(8,128)S(1)}, f32[1024,512]{1,0:T(8,128)}, u32[]{:S(2)}) copy-start(f32[1024,512]{1,0:T(8,128)} %shard_map.274) | copy-start | bytes 6291460
  180.7 3.6 copy-start
  187.7 1.6 copy-start.2
  187.7 4.6 %collective-permute-start.7 = (f32[1024,512]{1,0:T(8,128)}, f32[1024,512]{1,0:T(8,128)}, u32[]{:S(2)}, u32[]{:S(2)}) collective-permute-start(f32[1024,512]{1,0:T(8,128)} %get-tuple-element.58), channel_id=1, source_target_pairs={{0,1},{1,0},{2,3},{3,2},{4,5},{5,4},{6,7},{7,6},{8,9},{9,8},{10,11... | collective-permute-start | bytes 6291464 | tf_op jit(solution)/shard_map/ppermute | solution.py:544
  189.3 132.2 %collective-permute-start.5 = (f32[1024,512]{1,0:T(8,128)S(1)}, f32[1024,512]{1,0:T(8,128)}, u32[]{:S(2)}, u32[]{:S(2)}) collective-permute-start(f32[1024,512]{1,0:T(8,128)S(1)} %copy-done.2), channel_id=1, source_target_pairs={{0,1},{1,0},{2,3},{3,2},{4,5},{5,4},{6,7},{7,6},{8,9},{9,8},{10,11... | collective-permute-start | bytes 6291464 | tf_op jit(solution)/shard_map/ppermute | solution.py:544
  192.3 6.1 %copy-start.12 = (f32[8,512]{1,0:T(8,128)S(1)}, f32[8,512]{1,0:T(8,128)}, u32[]{:S(2)}) copy-start(f32[8,512]{1,0:T(8,128)} %get-tuple-element.66) | copy-start | bytes 49156
  192.3 51.4 %copy-start.10 = (f32[256,2]{1,0:T(8,128)S(1)}, f32[256,2]{1,0:T(8,128)}, u32[]{:S(2)}) copy-start(f32[256,2]{1,0:T(8,128)} %get-tuple-element.61) | copy-start | bytes 6148
  197.1 128.1 %collective-permute-start.8 = (f32[1024,512]{1,0:T(8,128)}, f32[1024,512]{1,0:T(8,128)}, u32[]{:S(2)}, u32[]{:S(2)}) collective-permute-start(f32[1024,512]{1,0:T(8,128)} %shard_map.269.own), channel_id=1, source_target_pairs={{0,1},{1,0},{2,3},{3,2},{4,5},{5,4},{6,7},{7,6},{8,9},{9,8},{10,11... | collective-permute-start | bytes 6291464 | tf_op jit(solution)/shard_map/ppermute | solution.py:544
  198.2 45.5 %collective-permute-start.11 = (f32[1024]{0:T(1024)S(1)}, f32[1024]{0:T(1024)S(1)}, u32[]{:S(2)}, u32[]{:S(2)}) collective-permute-start(f32[1024]{0:T(1024)S(1)} %bitcast.28), channel_id=1, source_target_pairs={{0,1},{1,0},{2,3},{3,2},{4,5},{5,4},{6,7},{7,6},{8,9},{9,8},{10,11... | collective-permute-start | bytes 12296 | tf_op jit(solution)/shard_map/ppermute | solution.py:544
  406.2 2.8 copy-start.9
  406.2 3.6 copy-start.5
  409.8 2.3 copy-start.4
Sparse Core Ops, SparseCore 0:
  187.8 218.3 all-reduce.5

commit v2 on v1

v2 whole, which is shorter than its diff:
```python
import functools
import math

import jax
import jax.numpy as jnp
from jax import lax
from jax.experimental import pallas as pl
from jax.experimental.pallas import tpu as pltpu
from jax.sharding import PartitionSpec as P

HD = 64
EPS = 1e-05
FAR = 1e30
f32 = jnp.float32
bf16 = jnp.bfloat16
QB = 512
QF = 256
PIECES = 16
LIMIT = 60 * 2**20


def dot(a, b, ca=1, cb=0):
    return lax.dot_general(a, b, (((ca,), (cb,)), ((), ())), preferred_element_type=f32)


def cost(flops, size):
    return pl.CostEstimate(flops=int(flops), bytes_accessed=int(size), transcendentals=0)


def shape(dims, kind=f32):
    return jax.ShapeDtypeStruct(dims, kind)


def whole(a):
    return pl.BlockSpec(a.shape, lambda *_: (0,) * len(a.shape))


def call(body, outs, scalars=(), arrays=(), in_specs=None, out_specs=None, grid=(1,), scratch=(), estimate=None, after=()):
    n, m = len(scalars) + len(arrays), len(after)
    outs = list(outs)

    def kernel(*refs):
        body(*refs[:n], *refs[n + m :])

    return pl.pallas_call(
        kernel,
        out_shape=outs,
        grid_spec=pltpu.PrefetchScalarGridSpec(
            num_scalar_prefetch=len(scalars),
            grid=grid,
            in_specs=[*(in_specs or [whole(a) for a in arrays]), *[pl.BlockSpec(memory_space=pl.ANY)] * m],
            out_specs=out_specs or [whole(o) for o in outs],
            scratch_shapes=list(scratch),
        ),
        compiler_params=pltpu.CompilerParams(vmem_limit_bytes=LIMIT),
        cost_estimate=estimate,
    )(*scalars, *arrays, *after)


def widen_kernel(*refs):
    count = len(refs) // 2
    for src, dst in zip(refs[:count], refs[count:]):
        dst[...] = src[...].astype(f32)


def widen(*arrays):
    return call(widen_kernel, [shape(a.shape) for a in arrays], arrays=arrays)


def turned_row(row):
    return jnp.broadcast_to(row, (8, row.shape[1])).T[:, 0:1]


def split3(v):
    high = v.astype(bf16)
    rest = v - high.astype(f32)
    mid = rest.astype(bf16)
    low = rest - mid.astype(f32)
    return high.astype(f32), mid.astype(f32), low


def tile_of(*given):
    row = lax.broadcasted_iota(jnp.int32, (16, given[0].shape[1]), 0)
    out = jnp.zeros(row.shape, f32)
    for j, v in enumerate(given):
        out = jnp.where(row == j, v, out)
    return out.astype(bf16)


def place_in(spans, shape_, base, axis):
    place = lax.broadcasted_iota(jnp.int32, shape_, axis) + base
    return jnp.where((place >= spans[0]) & (place < spans[1]), 1.0, 0.0)


def query_rows(spans, slots, base, count):
    cols = spans.astype(f32).T.astype(jnp.int32)
    inside = place_in((cols[:slots, 0:1], cols[:slots, 1:2]), (slots, count), base, 1)
    alone = 1.0 - jnp.sum(inside, axis=0, keepdims=True)
    return jnp.concatenate([(inside * -FAR).astype(bf16), tile_of(alone * -FAR)], axis=0)


def key_columns(spans, slots, base, count):
    inside = place_in((spans[0:1], spans[1:2]), (count, 128), base, 0)
    used = jnp.sum(inside, axis=1, keepdims=True)
    lane = lax.broadcasted_iota(jnp.int32, (count, 128), 1)
    ones = (lane > slots) & (lane < slots + 4)
    return jnp.where(
        lane < slots, 1.0 - inside, jnp.where(lane == slots, used, jnp.where(ones, 1.0, 0.0))
    )


def scaled_query(query):
    scaled = query.astype(f32) * (math.log2(math.e) / math.sqrt(HD))
    high = scaled.astype(bf16)
    return high, (scaled - high.astype(f32)).astype(bf16)


def forward_kernel(
    slots, me, tok_other, tok_own, weight, bias, spans,
    att_other, att_own, log_out, qt_out, kaug_out, seg_out, tokens, qhl, vt, segq, sbuf, mbuf,
):
    half = tok_other.shape[0]
    count = 2 * half
    heads = weight.shape[2] // HD
    tokens[0:half] = tok_other[...]
    tokens[half:count] = tok_own[...]
    bases = ((1 - me[0]) * half, me[0] * half)
    for part in range(2):
        at = slice(part * half, (part + 1) * half)
        segq[0 : slots + 16, at] = query_rows(spans[...], slots, bases[part], half)
    segq[slots + 16 :, :] = jnp.zeros((128 - slots - 16, count), bf16)
    seg_out[...] = segq[0 : slots + 16, :]
    bias_q, bias_v = turned_row(bias[0:1]), turned_row(bias[1:2])

    step = 512

    def project(i, carry):
        at = pl.multiple_of(i * step, step)
        rows = tokens[pl.ds(at, step), :]
        query = (dot(weight[0], rows, 0, 1) + bias_q).astype(bf16)
        qt_out[:, pl.ds(at, step)] = query
        high, low = scaled_query(query)
        value = (dot(weight[2], rows, 0, 1) + bias_v).astype(bf16)
        key = dot(rows, weight[1]).astype(bf16).astype(f32)
        base = jnp.where(at < half, bases[0], bases[1] - half) + at
        common = key_columns(spans[...], slots, base, step).astype(bf16)
        lane = lax.broadcasted_iota(jnp.int32, (step, 128), 1)
        for h in range(heads):
            qhl[h * 128 : h * 128 + HD, pl.ds(at, step)] = high[h * HD : (h + 1) * HD]
            qhl[h * 128 + HD : (h + 1) * 128, pl.ds(at, step)] = low[h * HD : (h + 1) * HD]
            vt[h * 80 : h * 80 + HD, pl.ds(at, step)] = value[h * HD : (h + 1) * HD]
            vt[h * 80 + HD : (h + 1) * 80, pl.ds(at, step)] = jnp.ones((16, step), bf16)
            if h % 2 == 0:
                pair = key[:, h * HD : h * HD + 128]
                turned = pltpu.roll(pair, HD, 1)
                twice = (jnp.where(lane < HD, pair, turned), jnp.where(lane < HD, turned, pair))
            kaug_out[h, pl.ds(at, step), 0:128] = twice[h % 2].astype(bf16)
            kaug_out[h, pl.ds(at, step), 128:256] = common
        return carry

    lax.fori_loop(0, count // step, project, 0)

    def score(h, at, slot):
        query = jnp.concatenate([qhl[h * 128 : (h + 1) * 128, pl.ds(at, QF)], segq[:, pl.ds(at, QF)]], axis=0)
        scores = dot(kaug_out[h], query)
        sbuf[slot] = scores
        mbuf[slot] = jnp.max(scores.reshape(count // 8, 8, QF), axis=0)

    def attend(h, at, out, place, slot):
        peak = jnp.max(mbuf[slot], axis=0, keepdims=True)
        probs = jnp.exp2(sbuf[slot] - peak).astype(bf16)
        summed = dot(vt[h * 80 : (h + 1) * 80, :], probs)
        total = summed[HD : HD + 1]
        out[h * HD : (h + 1) * HD, pl.ds(place, QF)] = summed[:HD] / total
        log_out[h : h + 1, pl.ds(at, QF)] = peak + jnp.log2(total)

    score(0, 0, 0)
    for part, out in enumerate((att_other, att_own)):

        def body(i, carry, part=part, out=out):
            place = pl.multiple_of(i * QF, QF)
            at = place + part * half
            for h in range(heads):
                if h + 1 < heads:
                    score(h + 1, at, (h + 1) % 2)
                else:
                    score(0, pl.multiple_of(jnp.minimum(at + QF, count - QF), QF), 0)
                attend(h, at, out, place, h % 2)
            return carry

        lax.fori_loop(0, half // QF, body, 0)


def halves_of(tokens):
    half, depth = tokens.shape[0] // 2, tokens.shape[1]
    return [
        pl.BlockSpec((half, depth), lambda i, me: (1 - me[0], 0)),
        pl.BlockSpec((half, depth), lambda i, me: (me[0], 0)),
    ]


def attend_forward(me, tokens, weight, bias, spans, slots):
    count, width = tokens.shape[0], weight.shape[2]
    half, heads, depth = count // 2, width // HD, tokens.shape[1]
    outs = [
        shape((width, half)),
        shape((width, half)),
        shape((8, count)),
        shape((width, count), bf16),
        shape((heads, count, 256), bf16),
        shape((slots + 16, count), bf16),
    ]
    rest = (weight, bias, spans)
    return call(
        functools.partial(forward_kernel, slots),
        outs,
        scalars=(me,),
        arrays=(tokens, tokens, *rest),
        in_specs=[*halves_of(tokens), *[whole(a) for a in rest]],
        scratch=[
            pltpu.VMEM((count, depth), bf16),
            pltpu.VMEM((heads * 128, count), bf16),
            pltpu.VMEM((heads * 80, count), bf16),
            pltpu.VMEM((128, count), bf16),
            pltpu.VMEM((2, count, QF), f32),
            pltpu.VMEM((2, 8, QF), f32),
        ],
        estimate=cost(20e9, 12e6),
    )


def norm(v):
    center = v - jnp.mean(v, axis=-1, keepdims=True)
    rstd = lax.rsqrt(jnp.mean(center * center, axis=-1, keepdims=True) + EPS)
    return center * rstd, rstd


def norm_back(grad, n, rstd):
    first = jnp.mean(grad, axis=-1, keepdims=True)
    second = jnp.mean(grad * n, axis=-1, keepdims=True)
    return rstd * (grad - first - n * second)


def normal_parts(h):
    size = jnp.abs(h)
    t = 1.0 / (1.0 + (0.3275911 * math.sqrt(0.5)) * size)
    bell = jnp.exp2(h * h * (-0.5 * math.log2(math.e)))
    poly = t * (
        0.127414796 + t * (-0.142248368 + t * (0.7107068705 + t * (-0.7265760135 + t * 0.5307027145)))
    )
    tail = poly * bell
    below = jnp.where(h < 0, tail, 1.0 - tail)
    return below, bell * (1.0 / math.sqrt(2.0 * math.pi))


def gather(ref, order, first, pieces):
    deep = ref.shape[0] // PIECES
    return jnp.concatenate(
        [ref[pl.ds(pl.multiple_of(order[first + r] * deep, deep), deep), :] for r in range(pieces)], axis=0
    )


def grad_lanes(grt, nlt, gbt, act, gh, att):
    return jnp.concatenate([dot(grt, act), dot(nlt, gh), dot(gbt, att, 1, 1)], axis=1)


def middle_kernel(
    order, me, att_own, att_rcv, wo_own, wo_rcv, we_own, we_rcv, wr_own, wr_rcv, eb_own, eb_rcv,
    tok, cot, rows, spans,
    layer_out, resid_out, ga_own, ga_other, act_out, gh_out, nlt_out, grt_out, gbt_out, att_out, small,
    keep_out, send_out, wo, we, wr, act_s, gh_s, nlt_s, grt_s, gbt_s, att_s,
):
    i = pl.program_id(0)
    steps = pl.num_programs(0) - 2
    units = we_own.shape[1]
    width = wo_own.shape[0]
    count, depth = tok.shape

    @pl.when(i == 0)
    def _():
        wo[0:width] = wo_own[...]
        wo[width:] = wo_rcv[...].astype(bf16)
        we[:, 0:units] = we_own[...]
        we[:, units:] = we_rcv[...].astype(bf16)
        wr[0:units] = wr_own[...]
        wr[units:] = wr_rcv[...].astype(bf16)
        small[...] = jnp.zeros_like(small)

    @pl.when(i < steps)
    def _():
        output_bias, gain1, shift1, reduce_bias, gain2, shift2 = (rows[j : j + 1] for j in range(6))
        base = (me[0] * steps + i) * count
        inside = place_in((spans[0:1], spans[1:2]), (count, 128), base, 0)
        valid = jnp.sum(inside, axis=1, keepdims=True)
        here = pl.ds(pl.multiple_of(i * count, count), count)

        att = jnp.concatenate([att_own[...], att_rcv[...]], axis=0).astype(bf16)
        att_out[...] = att[:width]
        att_s[:, here] = att[width:]
        resid_one = tok[...].astype(f32) + (dot(att, wo[...], 0, 0) + output_bias)
        n1, rstd1 = norm(resid_one)
        normed = n1 * gain1 + shift1
        normed_low = normed.astype(bf16)
        turned = normed_low.T
        nlt_out[...] = turned
        nlt_s[:, here] = turned
        bias = jnp.concatenate([eb_own[...], eb_rcv[...]], axis=1)
        hidden = dot(normed_low, we[...]) + bias
        below, density = normal_parts(hidden)
        active = (hidden * below).astype(bf16)
        slope = below + hidden * density
        act_out[...] = active[:, :units]
        act_s[here, :] = active[:, units:]
        resid_two = normed + (dot(active, wr[...]) + reduce_bias)
        n2, rstd2 = norm(resid_two)
        layer_out[...] = ((n2 * gain2 + shift2) * valid).astype(bf16).astype(f32)
        grad = cot[...].astype(f32) * valid
        column = lambda v: jnp.sum(v, axis=0, keepdims=True)
        small[0:1, :depth] += column(grad * n2)
        small[1:2, :depth] += column(grad)
        grad_two = norm_back(grad * gain2, n2, rstd2)
        grad_result = grad_two.astype(bf16)
        turned = grad_result.T
        grt_out[...] = turned
        grt_s[:, here] = turned
        small[2:3, :depth] += column(grad_result.astype(f32))
        grad_hidden = (dot(grad_result, wr[...], 1, 1) * slope).astype(bf16)
        gh_out[...] = grad_hidden[:, :units]
        gh_s[here, :] = grad_hidden[:, units:]
        small[6:7] += column(grad_hidden.astype(f32))
        grad_normed = grad_two + dot(grad_hidden, we[...], 1, 1)
        small[3:4, :depth] += column(grad_normed * n1)
        small[4:5, :depth] += column(grad_normed)
        grad_one = norm_back(grad_normed * gain1, n1, rstd1)
        resid_out[...] = grad_one
        grad_branch = grad_one.astype(bf16)
        turned = grad_branch.T
        gbt_out[...] = turned
        gbt_s[:, here] = turned
        small[5:6, :depth] += column(grad_branch.astype(f32))
        grad_att = dot(wo[...], grad_branch, 1, 1).astype(bf16).astype(f32)
        ga_own[...] = grad_att[0:width]
        ga_other[...] = grad_att[width:]

    for first, out in ((0, keep_out), (PIECES // 2, send_out)):

        @pl.when(i == steps + first // (PIECES // 2))
        def _(first=first, out=out):
            parts = [gather(ref, order, first, PIECES // 2) for ref in (grt_s, nlt_s, gbt_s)]
            wide = out.shape[1] // 2
            for j in range(2):
                u = slice(j * units // 2, (j + 1) * units // 2)
                e = slice(j * width // 2, (j + 1) * width // 2)
                out[:, j * wide : (j + 1) * wide] = grad_lanes(*parts, act_s[:, u], gh_s[:, u], att_s[e, :])


def middle(order, me, att_own, att_rcv, weights, tokens, cotangent, rows, spans):
    half, depth = tokens.shape[0] // 2, tokens.shape[1]
    width, units = weights[0].shape[0], weights[2].shape[1]
    blk = 256
    steps = half // blk
    at = lambda i: jnp.minimum(i, steps - 1)
    by_row = lambda n: pl.BlockSpec((blk, n), lambda i, *_: (at(i), 0))
    by_col = lambda n: pl.BlockSpec((n, blk), lambda i, *_: (0, at(i)))
    mine = pl.BlockSpec((blk, depth), lambda i, order, me: (me[0] * steps + at(i), 0))
    lanes = 2 * units + width
    outs = [
        (shape((half, depth)), by_row(depth)),
        (shape((half, depth)), by_row(depth)),
        (shape((width, half)), by_col(width)),
        (shape((width, half)), by_col(width)),
        (shape((half, units), bf16), by_row(units)),
        (shape((half, units), bf16), by_row(units)),
        (shape((depth, half), bf16), by_col(depth)),
        (shape((depth, half), bf16), by_col(depth)),
        (shape((depth, half), bf16), by_col(depth)),
        (shape((width, half), bf16), by_col(width)),
        (shape((8, 2 * units)), None),
        (shape((depth // 2, lanes)), None),
        (shape((depth // 2, lanes)), None),
    ]
    return call(
        middle_kernel,
        [o for o, _ in outs],
        scalars=(order, me),
        arrays=(att_own, att_rcv, *weights, tokens, cotangent, rows, spans),
        in_specs=[
            by_col(width),
            by_col(width),
            *[whole(a) for a in weights],
            mine,
            mine,
            whole(rows),
            whole(spans),
        ],
        out_specs=[s or whole(o) for o, s in outs],
        grid=(steps + 2,),
        scratch=[
            pltpu.VMEM((2 * width, depth), bf16),
            pltpu.VMEM((depth, 2 * units), bf16),
            pltpu.VMEM((2 * units, depth), bf16),
            pltpu.VMEM((half, units), bf16),
            pltpu.VMEM((half, units), bf16),
            pltpu.VMEM((depth, half), bf16),
            pltpu.VMEM((depth, half), bf16),
            pltpu.VMEM((depth, half), bf16),
            pltpu.VMEM((width, half), bf16),
        ],
        estimate=cost(20e9, 40e6),
    )


def own_grads_kernel(first, order, grt, nlt, gbt, act, gh, att, got, out):
    parts = [gather(ref, order, first, PIECES // 2) for ref in (grt, nlt, gbt)]
    out[...] = grad_lanes(*parts, act[...], gh[...], att[...]) + got[...]


def own_grads(first, order, grt, nlt, gbt, act, gh, att, got):
    half, units, width = act.shape[0], act.shape[1], att.shape[0]
    rows, lanes = got.shape
    part = pl.BlockSpec((half, units // 2), lambda i, order: (0, i))
    block = pl.BlockSpec((rows, lanes // 2), lambda i, order: (0, i))
    return call(
        functools.partial(own_grads_kernel, first),
        [shape(got.shape)],
        scalars=(order,),
        arrays=(grt, nlt, gbt, act, gh, att, got),
        in_specs=[
            *[whole(a) for a in (grt, nlt, gbt)],
            part,
            part,
            pl.BlockSpec((width // 2, half), lambda i, order: (i, 0)),
            block,
        ],
        out_specs=[block],
        grid=(2,),
        estimate=cost(3e9, 10e6),
    )[0]


def place_grads_kernel(order, low, high, reduce, expand, out, red, outt):
    deep = expand.shape[0] // PIECES
    units, width = red.shape[1] // 2, outt.shape[1] // 2
    for r in range(PIECES):
        src = (low, high)[r // (PIECES // 2)]
        of = slice(r % (PIECES // 2) * deep, r % (PIECES // 2) * deep + deep)
        at = pl.ds(pl.multiple_of(order[r] * deep, deep), deep)
        for j in range(2):
            lane = j * (src.shape[1] // 2)
            for dst, wide in ((red, units), (expand, units), (outt, width)):
                dst[at, j * wide : (j + 1) * wide] = src[of, lane : lane + wide]
                lane += wide
    reduce[...] = red[...].T
    out[...] = outt[...].T


def place_grads(order, low, high, units, width):
    depth = 2 * low.shape[0]
    return call(
        place_grads_kernel,
        [shape((units, depth)), shape((depth, units)), shape((width, depth))],
        scalars=(order,),
        arrays=(low, high),
        scratch=[pltpu.VMEM((depth, units), f32), pltpu.VMEM((depth, width), f32)],
        estimate=cost(0, 10e6),
    )


def prepare_kernel(me, tok_other, tok_own, weight, bias, kt, vaug, tokt):
    half = tok_other.shape[0]
    heads = weight.shape[2] // HD
    lane = lax.broadcasted_iota(jnp.int32, (half, 128), 1)
    ones = jnp.where(lane < HD + 3, 1.0, 0.0)
    for part, tok in enumerate((tok_other, tok_own)):
        at = slice(part * half, (part + 1) * half)
        tokt[:, at] = tok[...].T
        kt[:, at] = dot(weight[1], tok[...], 0, 1).astype(bf16)
        value = (dot(tok[...], weight[2]) + bias[1:2]).astype(bf16).astype(f32)
        for h in range(heads):
            pair = value[:, h // 2 * 128 : h // 2 * 128 + 128]
            if h % 2:
                pair = pltpu.roll(pair, HD, 1)
            vaug[h, at, :] = jnp.where(lane < HD, pair, ones).astype(bf16)


def prepare(me, tokens, weight, bias, after):
    count, depth = tokens.shape
    width = weight.shape[2]
    return call(
        prepare_kernel,
        [shape((width, count), bf16), shape((width // HD, count, 128), bf16), shape((depth, count), bf16)],
        scalars=(me,),
        arrays=(tokens, tokens, weight, bias),
        in_specs=[*halves_of(tokens), whole(weight), whole(bias)],
        estimate=cost(4e9, 8e6),
        after=after,
    )


def backward_kernel(
    head, qt, kt, kaug, vaug, seg, logs, att_other, att_own, ga_other, ga_own, dq, dk, dv, dkt, dvt
):
    half = att_other.shape[1]
    slots = seg.shape[0] - 16
    scale = HD**-0.5
    dkt[...] = jnp.zeros_like(dkt)
    dvt[...] = jnp.zeros_like(dvt)
    zeros_q = jnp.zeros((256 - 2 * HD - slots - 16, QB), bf16)
    zeros_v = jnp.zeros((128 - HD - 16, QB), bf16)

    for part, (att, ga) in enumerate(((att_other, ga_other), (att_own, ga_own))):

        def body(i, carry, part=part, att=att, ga=ga):
            place = pl.multiple_of(i * QB, QB)
            at = place + part * half
            grad = ga[:, pl.ds(place, QB)]
            inner = -jnp.sum(grad * att[:, pl.ds(place, QB)], axis=0, keepdims=True)
            grad_low = grad.astype(bf16)
            upper = jnp.concatenate([grad_low, tile_of(*split3(inner)), zeros_v], axis=0)
            query = qt[:, pl.ds(at, QB)]
            logs_q = logs[head : head + 1, pl.ds(at, QB)]
            alone = seg[slots : slots + 1, pl.ds(at, QB)].astype(f32)
            tile = tile_of(alone, *split3(-logs_q))
            left = jnp.concatenate([*scaled_query(query), seg[0:slots, pl.ds(at, QB)], tile, zeros_q], axis=0)
            probs = jnp.exp2(dot(kaug[0], left))
            grad_probs = dot(vaug[0], upper)
            grad_scores = (probs * grad_probs).astype(bf16)
            dvt[...] += dot(grad_low, probs.astype(bf16), 1, 1)
            dkt[...] += dot(query, grad_scores, 1, 1)
            dq[:, pl.ds(at, QB)] = (dot(kt[...], grad_scores) * scale).astype(bf16)
            return carry

        lax.fori_loop(0, half // QB, body, 0)
    dk[...] = (dkt[...] * scale).astype(bf16)
    dv[...] = dvt[...].astype(bf16)


def attend_backward(head, qt, kt, kaug, vaug, seg, logs, att_other, att_own, ga_other, ga_own, after):
    count = qt.shape[1]
    by_head = lambda n: pl.BlockSpec((HD, n), lambda i: (head, 0))
    return call(
        functools.partial(backward_kernel, head),
        [shape((HD, count), bf16)] * 3,
        arrays=(qt, kt, kaug, vaug, seg, logs, att_other, att_own, ga_other, ga_own),
        in_specs=[
            by_head(count),
            by_head(count),
            pl.BlockSpec((1, count, 256), lambda i: (head, 0, 0)),
            pl.BlockSpec((1, count, 128), lambda i: (head, 0, 0)),
            whole(seg),
            whole(logs),
            *[by_head(count // 2)] * 4,
        ],
        scratch=[pltpu.VMEM((HD, count), f32), pltpu.VMEM((HD, count), f32)],
        estimate=cost(13e9, 6e6),
        after=after,
    )


def project_grad_kernel(order, tokt, small, small_rcv, *refs):
    *parts, keep, send, full = refs
    rows, lanes = keep.shape
    units, depth = small.shape[1] // 2, tokt.shape[0]
    width = lanes // 3
    for j, part in enumerate(parts):
        full[j * HD : (j + 1) * HD] = part[...]
    for first, out in ((0, keep), (PIECES // 2, send)):
        out[: rows - 16] = dot(gather(tokt, order, first, PIECES // 2), full[...], 1, 1)
        out[rows - 16 :] = jnp.zeros((16, lanes), f32)
        out[rows - 16 : rows - 10, :depth] = small[0:6, :depth] + small_rcv[0:6, :depth]
        hidden = small[6:7, :units] + small_rcv[6:7, units:]
        for j in range(units // depth):
            out[rows - 10 + j : rows - 9 + j, :depth] = hidden[:, j * depth : (j + 1) * depth]
        column = dot(jnp.ones((8, full.shape[1]), bf16), full[...], 1, 1)
        out[rows - 8 : rows - 7, 0:width] = column[0:1, 0:width]
        out[rows - 8 : rows - 7, width : 2 * width] = column[0:1, 2 * width :]


def project_grad(order, tokt, small, small_rcv, parts):
    depth, count = tokt.shape
    lanes = len(parts) * HD
    return call(
        project_grad_kernel,
        [shape((depth // 2 + 16, lanes))] * 2,
        scalars=(order,),
        arrays=(tokt, small, small_rcv, *parts),
        scratch=[pltpu.VMEM((lanes, count), bf16)],
        estimate=cost(4e9, 8e6),
    )


def project_rows_kernel(weight, *refs):
    *parts, other, own, full = refs
    half = other.shape[1]
    width = weight.shape[2]
    for j, part in enumerate(parts):
        full[j * HD : (j + 1) * HD] = part[...]
    for at, out in ((0, other), (half, own)):
        out[...] = sum(
            dot(weight[c], full[c * width : (c + 1) * width, at : at + half]) for c in range(weight.shape[0])
        )


def project_rows(weight, parts, after):
    depth, count = weight.shape[1], parts[0].shape[1]
    return call(
        project_rows_kernel,
        [shape((depth, count // 2))] * 2,
        arrays=(weight, *parts),
        scratch=[pltpu.VMEM((len(parts) * HD, count), bf16)],
        estimate=cost(4e9, 8e6),
        after=after,
    )


def place_attend_kernel(order, low, high, small, out, bias, hidden, *vectors):
    deep = out.shape[1] // PIECES
    width = out.shape[2]
    depth = out.shape[1]
    for r in range(PIECES):
        src = (low, high)[r // (PIECES // 2)]
        of = slice(r % (PIECES // 2) * deep, r % (PIECES // 2) * deep + deep)
        at = pl.ds(pl.multiple_of(order[r] * deep, deep), deep)
        for c in range(3):
            out[c, at, :] = src[of, c * width : (c + 1) * width]
    bias[0:1] = small[8:9, 0:width]
    bias[1:2] = small[8:9, width : 2 * width]
    for j in range(hidden.shape[1] // depth):
        hidden[:, j * depth : (j + 1) * depth] = small[6 + j : 7 + j, :depth]
    for j, vector in enumerate(vectors):
        vector[...] = small[j : j + 1, :depth]


def place_attend(order, low, high, small, depth, width, units):
    return call(
        place_attend_kernel,
        [shape((3, depth, width)), shape((2, width)), shape((1, units)), *[shape((1, depth))] * 6],
        scalars=(order,),
        arrays=(low, high, small),
        estimate=cost(0, 6e6),
    )


def add_rows_kernel(a, b, c, out):
    out[...] = ((a[...] + b[...]).T + c[...]).astype(bf16).astype(f32)


def add_rows(a, b, c):
    rows, depth = c.shape
    turned = pl.BlockSpec((depth, rows // 4), lambda i: (0, i))
    blk = pl.BlockSpec((rows // 4, depth), lambda i: (i, 0))
    return call(
        add_rows_kernel,
        [shape(c.shape)],
        arrays=(a, b, c),
        grid=(4,),
        in_specs=[turned, turned, blk],
        out_specs=[blk],
        estimate=cost(0, 8e6),
    )[0]


def join_kernel(me, own, other, out):
    mine = pl.program_id(0) == me[0]

    @pl.when(mine)
    def _():
        out[...] = own[...].astype(bf16)

    @pl.when(jnp.logical_not(mine))
    def _():
        out[...] = other[...].astype(bf16)


def join(me, own, other, after=()):
    half, depth = own.shape
    block = pl.BlockSpec((half, depth), lambda i, me: (0, 0))
    return call(
        join_kernel,
        [shape((2 * half, depth), bf16)],
        scalars=(me,),
        arrays=(own, other),
        grid=(2,),
        in_specs=[block, block],
        out_specs=[pl.BlockSpec((half, depth), lambda i, me: (i, 0))],
        estimate=cost(0, 6e6),
        after=after,
    )[0]


def swap(v):
    return lax.ppermute(v, "mp", [(0, 1), (1, 0)])


BITS = ((1, 2), (2, 1), (4, 4), (8, 8))


def masks(core):
    return [sum(BITS[3 - b][core] for b in range(4) if r >> b & 1) for r in range(PIECES)]


def piece_order(which):
    table = jnp.array([masks(0), masks(1)], jnp.int32)
    core = lax.axis_index("mp")
    return lax.axis_index("dp").astype(jnp.int32) ^ table[1 - core if which else core]


def across(v, position):
    pairs = [
        (2 * d + core, 2 * (d ^ masks(core)[position]) + core) for d in range(PIECES) for core in range(2)
    ]
    return lax.ppermute(v, ("dp", "mp"), pairs)


def halve_first(keep, send, extra=0):
    got = across(send, 8)
    half = (keep.shape[0] - extra) // 2
    lead = keep[half:] + got[half:]
    return lead, keep[:half] + got[:half]


def halve_second(lead, rest, extra=0):
    got = across(lead, 4)
    half = rest.shape[0]
    mine = rest + got[:half]
    return mine, lead[half:] + got[half:]


def halve_last(mine, more, extra=0):
    size = mine.shape[0] // 4
    got = []
    for p in (3, 2, 1):
        part = mine[p * size : (p + 1) * size]
        got.append(across(jnp.concatenate([part, more]) if extra else part, p))
    piece = mine[:size] + got[0][:size] + got[1][:size] + got[2][:size]
    return piece, more + got[0][size:] + got[1][size:] + got[2][size:]


def double_first(piece):
    got = [across(piece, p) for p in (3, 2, 1)]
    return jnp.concatenate([piece, got[2], got[1], got[0]])


def double_second(four):
    return jnp.concatenate([four, across(four, 4)])


def local(
    tokens, seq_starts, seq_lengths, attend_weight, attend_bias, output_weight, output_bias, first_gain, first_shift,
    expand_weight, expand_bias, reduce_weight, reduce_bias, second_gain, second_shift, cotangent,
):
    slots = seq_starts.shape[1]
    units, width, depth = expand_weight.shape[1], output_weight.shape[0], tokens.shape[1]
    by_pieces = lax.axis_size("dp") == PIECES
    me = lax.axis_index("mp").astype(jnp.int32)[None]
    plain = jnp.arange(PIECES, dtype=jnp.int32)
    order, order_other = (piece_order(0), piece_order(1)) if by_pieces else (plain, plain)
    spans = jnp.concatenate([seq_starts, seq_starts + seq_lengths])
    spans = jnp.pad(spans, ((0, 6), (0, 128 - slots)))
    eb_own = expand_bias[None, :]
    wide = widen(output_weight, expand_weight, reduce_weight)
    wo_rcv, we_rcv, wr_rcv = (swap(w) for w in wide)
    eb_rcv = swap(eb_own)
    rows = jnp.stack(
        [output_bias, first_gain, first_shift, reduce_bias, second_gain, second_shift, first_gain, first_gain]
    )

    att_other, att_own, logs, qt, kaug, seg = attend_forward(me, tokens, attend_weight, attend_bias, spans, slots)
    att_rcv = swap(att_other)
    weights = (output_weight, wo_rcv, expand_weight, we_rcv, reduce_weight, wr_rcv, eb_own, eb_rcv)
    (layer_own, resid, ga_own, ga_other, act, gh, nlt, grt, gbt, att, small, keep, send) = middle(
        order_other, me, att_own, att_rcv, weights, tokens, cotangent, rows, spans
    )
    send_rcv, keep_rcv, ga_rcv = swap(send), swap(keep), swap(ga_other)
    small_rcv, layer_rcv = swap(small), swap(layer_own)
    kt, vaug, tokt = prepare(me, tokens, attend_weight, attend_bias, (small,))
    send = own_grads(PIECES // 2, order, grt, nlt, gbt, act, gh, att, send_rcv)
    keep = own_grads(0, order, grt, nlt, gbt, act, gh, att, keep_rcv)

    def backward(h, after):
        return attend_backward(h, qt, kt, kaug, vaug, seg, logs, att_other, att_own, ga_rcv, ga_own, after)

    heads = [backward(0, (keep,)), backward(1, (keep,))]
    if by_pieces:
        lead, rest = halve_first(keep, send)
        heads.append(backward(2, (lead,)))
        mine, more = halve_second(lead, rest)
        heads.append(backward(3, (mine,)))
        piece, _ = halve_last(mine, more)
    else:
        heads += [backward(2, ()), backward(3, ())]
    parts = [head[c] for c in range(3) for head in heads]
    keep_a, send_a = project_grad(order, tokt, small, small_rcv, parts)
    rows_other, rows_own = project_rows(attend_weight, parts, (keep_a,))
    rows_rcv = swap(rows_other)
    mine_rows = add_rows(rows_own, rows_rcv, resid)
    rows_back = swap(mine_rows)

    if by_pieces:
        four = double_first(piece)
        lead_a, rest_a = halve_first(keep_a, send_a, 16)
        mine_a, more_a = halve_second(lead_a, rest_a, 16)
        piece_a, totals = halve_last(mine_a, more_a, 16)
        low = double_second(four)
        four_a = double_first(piece_a)
        high = across(low, 8)
        low_a = double_second(four_a)
        high_a = across(low_a, 8)
    else:
        low, high, low_a, high_a = lax.psum((keep, send, keep_a, send_a), "dp")
        totals = low_a[-16:]
    grad_tokens = join(me, mine_rows, rows_back)
    layer_out = join(me, layer_own, layer_rcv)
    grad_reduce, grad_expand, grad_output = place_grads(order, low, high, units, width)
    grad_attend, grad_bias, grad_hidden, *vectors = place_attend(order, low_a, high_a, totals, depth, width, units)
    vectors = [v.reshape(depth) for v in vectors]
    return (
        layer_out,
        grad_tokens,
        grad_attend,
        grad_bias,
        grad_output,
        vectors[5],
        vectors[3],
        vectors[4],
        grad_expand,
        grad_hidden.reshape(units),
        grad_reduce,
        vectors[2],
        vectors[0],
        vectors[1],
    )


def solution(mesh):
    return jax.shard_map(
        local,
        mesh=mesh,
        in_specs=(
            P("dp", None),
            P("dp", None),
            P("dp", None),
            P(None, None, "mp"),
            P(None, "mp"),
            P("mp", None),
            P(),
            P(),
            P(),
            P(None, "mp"),
            P("mp"),
            P("mp", None),
            P(),
            P(),
            P(),
            P("dp", None),
        ),
        out_specs=(
            P("dp", None),
            P("dp", None),
            P(None, None, "mp"),
            P(None, "mp"),
            P("mp", None),
            P(),
            P(),
            P(),
            P(None, "mp"),
            P("mp"),
            P("mp", None),
            P(),
            P(),
            P(),
        ),
        check_vma=False,
    )
```

time: 421 us -> 292 us (0.69); the launches traced: 420 us -> 286 us
  blocking collectives: 122 us -> 0 us
  starting transfers between devices: 3.79 us -> 29.3 us
  between operations: 14.2 us -> 1.42 us
  waiting for transfers between devices: 82 us -> 70.5 us
  local copies, waits for them, and re-layouts: 17.6 us -> 6.25 us
    psum x2 -> x0, blocking collectives: 122 us -> none  [the longest x1 77.1 us: local(): grad_attbias, grad_expbias = lax.psum((bias_grad.T, eb_sum), 'dp')]
    psum x1 -> x0, waiting for transfers between devices: 77.1 us -> none  [local(): lax.psum((grad_attend, grad_output, grad_expand, grad_reduce), 'dp')]
    ppermute x0 -> x20, waiting for transfers between devices: none -> 68.9 us  [across(): return lax.ppermute(v, ('dp', 'mp'), pairs)]
    ppermute x0 -> x20, starting transfers between devices: none -> 26.3 us  [across(): return lax.ppermute(v, ('dp', 'mp'), pairs)]
    unnamed x53 -> x50, local copies, waits for them, and re-layouts: 11.8 us -> 4.83 us
    pallas_call x13 -> x17, Pallas kernels: 173 us -> 171 us  [call(): pl.pallas_call(kernel, out_shape=outs, grid_spec=pltpu.PrefetchScalarGrid...]
  transfers between devices with their start and end apart: 14 -> 32, of which waited for: 4 -> 16; matrix products, arithmetic and copies ran while one was open for 3% -> 3% of each run, Pallas kernels for 33% -> 46%
where the time goes in v2:
time: 292 us; the launch traced here: 286 us
  Pallas kernels  171 us (59%)
  waiting for transfers between devices  70.5 us (24%)
  starting transfers between devices  29.3 us (10%)
  other arithmetic  7.72 us (3%)
  local copies, waits for them, and re-layouts  6.25 us (2%)
    pallas_call x17, Pallas kernels, call(): pl.pallas_call(kernel, out_shape=outs, grid_spec=pltpu.PrefetchScalarGrid...  171 us
    ppermute x20, waiting for transfers between devices, across(): return lax.ppermute(v, ('dp', 'mp'), pairs)  68.9 us
    ppermute x20, starting transfers between devices, across(): return lax.ppermute(v, ('dp', 'mp'), pairs)  26.3 us
  transfers between devices with their start and end apart: 32, of which 16 were waited for; matrix products, arithmetic and copies ran while one was open for 3% of the time, Pallas kernels for 46%

profile of v2, /device:TPU:0, one launch (start us, length us, event | category | flops | bytes accessed | tf_op | source)
XLA Modules:
  0.0 286.2 jit_solution(16508943852615190811)
XLA Ops:
  0.7 3.9 %shard_map.282 = (f32[256,512]{1,0:T(8,128)}, f32[512,1024]{1,0:T(8,128)}, f32[1024,512]{1,0:T(8,128)}) custom-call(bf16[256,512]{1,0:T(8,128)(2,1)} %refs_4_.4, bf16[512,1024]{1,0:T(8,128)(2,1)} %refs_6_.1, bf16[1024,512]{1,0:T(8,128)(2,1)} %refs_8_.1), custom_call_target="tpu_custom_call" | custom-call | tf_op jit(solution)/shard_map/pallas_call | solution.py:45
  5.8 25.7 %shard_map.281 = (f32[256,1024]{1,0:T(8,128)}, f32[256,1024]{1,0:T(8,128)}, f32[8,2048]{1,0:T(8,128)}, bf16[256,2048]{1,0:T(8,128)(2,1)}, bf16[4,2048,256]{2,1,0:T(8,128)(2,1)}, /*index=5*/bf16[32,2048]{1,0:T(8,128)(2,1)}) custom-call(s32[1]{0:T(128)} %bitcast.refs_0_.refs_1_, bf16[2048,512]{1,0:T(8,128)(2,1)} %refs_2_.5, bf16[2048,512]{1,0:T(8,128)(2,1)} %refs_2_.5, ...), custom_call_target="tpu_custom_call" | custom-call | flops 20000000000 | bytes 12000000 | tf_op jit(solution)/shard_map/pallas_call | solution.py:45
  33.7 1.2 collective-permute-done.4.refs_11_
  37.0 31.6 %shard_map.283 = (f32[1024,512]{1,0:T(8,128)}, f32[1024,512]{1,0:T(8,128)}, f32[256,1024]{1,0:T(8,128)}, f32[256,1024]{1,0:T(8,128)}, bf16[1024,1024]{1,0:T(8,12...) custom-call(s32[16]{0:T(128)} %get-tuple-element.134.refs_0_, ...), custom_call_target="tpu_custom_call" | custom-call | flops 20000000000 | bytes 40000000 | tf_op jit(solution)/shard_map/pallas_call | solution.py:45
  70.0 5.5 %shard_map.285 = (bf16[256,2048]{1,0:T(8,128)(2,1)}, bf16[4,2048,128]{2,1,0:T(8,128)(2,1)}, bf16[512,2048]{1,0:T(8,128)(2,1)}) custom-call(s32[1]{0:T(128)} %bitcast.refs_0_.refs_1_, bf16[2048,512]{1,0:T(8,128)(2,1)} %refs_2_.5, bf16[2048,512]{1,0:T(8,128)(2,1)} %refs_2_.5, bf16[3,512,256]{2,1,0:T(8,128)(2,1)} %refs_0_.3, f32[2,256]{1,0:T(2,128)} %refs_4_.5, ...), custom_call_target="tpu_custom_call" | custom-call | flops 4000000000 | bytes 8000000 | tf_op jit(solution)/shard_map/pallas_call | solution.py:45
  75.6 6.7 %shard_map.289 = f32[256,2304]{1,0:T(8,128)} custom-call(s32[16]{0:T(128)} %get-tuple-element.133.refs_0_, bf16[512,1024]{1,0:T(8,128)(2,1)} %get-tuple-element.82.refs_1_, bf16[512,1024]{1,0:T(8,128)(2,1)} %get-tuple-element.83.refs_2_, bf16[512,1024]{1,0:T(8,128)(2,1)} %get-tuple-element.84.refs_3_, bf16[1024,1024]{1,0:T(8,128)(2,1)} %get-tuple-element.85.refs_4_, ...), custom_call_target="tpu_custom_call" | custom-call | flops 3000000000 | bytes 10000000 | tf_op jit(solution)/shard_map/pallas_call | solution.py:45
  82.2 2.6 collective-permute-start.9
  84.9 1.4 copy-done.3
  86.3 6.7 %shard_map.286.refs_10_ = f32[256,2304]{1,0:T(8,128)} custom-call(s32[16]{0:T(128)} %get-tuple-element.133.refs_0_, bf16[512,1024]{1,0:T(8,128)(2,1)} %get-tuple-element.82.refs_1_, bf16[512,1024]{1,0:T(8,128)(2,1)} %get-tuple-element.83.refs_2_, bf16[512,1024]{1,0:T(8,128)(2,1)} %get-tuple-element.84.refs_3_, bf16[1024,1024]{1,0:T(8,128)(2,1)} %get-tuple-element.85.refs_4_, ...), custom_call_target="tpu_custom_call" | custom-call | flops 3000000000 | bytes 10000000 | tf_op jit(solution)/shard_map/pallas_call | solution.py:45
  93.0 1.0 copy-done.16
  94.0 14.4 %shard_map.288 = (bf16[64,2048]{1,0:T(8,128)(2,1)}, bf16[64,2048]{1,0:T(8,128)(2,1)}, bf16[64,2048]{1,0:T(8,128)(2,1)}) custom-call(bf16[256,2048]{1,0:T(8,128)(2,1)} %get-tuple-element.73.refs_0_, bf16[256,2048]{1,0:T(8,128)(2,1)} %get-tuple-element.75.refs_1_, bf16[4,2048,256]{2,1,0:T(8,128)(2,1)} %get-tuple-element.76.refs_2_, ...), custom_call_target="tpu_custom_call" | custom-call | flops 12999999488 | bytes 6000000 | tf_op jit(solution)/shard_map/pallas_call | solution.py:45
  108.4 14.3 %shard_map.287 = (bf16[64,2048]{1,0:T(8,128)(2,1)}, bf16[64,2048]{1,0:T(8,128)(2,1)}, bf16[64,2048]{1,0:T(8,128)(2,1)}) custom-call(bf16[256,2048]{1,0:T(8,128)(2,1)} %get-tuple-element.73.refs_0_, bf16[256,2048]{1,0:T(8,128)(2,1)} %get-tuple-element.75.refs_1_, bf16[4,2048,256]{2,1,0:T(8,128)(2,1)} %get-tuple-element.76.refs_2_, ...), custom_call_target="tpu_custom_call" | custom-call | flops 12999999488 | bytes 6000000 | tf_op jit(solution)/shard_map/pallas_call | solution.py:45
  122.7 1.4 slice_add_fusion.1.refs_10_
  124.1 1.7 collective-permute-start.10
  125.8 14.4 %shard_map.290 = (bf16[64,2048]{1,0:T(8,128)(2,1)}, bf16[64,2048]{1,0:T(8,128)(2,1)}, bf16[64,2048]{1,0:T(8,128)(2,1)}) custom-call(bf16[256,2048]{1,0:T(8,128)(2,1)} %get-tuple-element.73.refs_0_, bf16[256,2048]{1,0:T(8,128)(2,1)} %get-tuple-element.75.refs_1_, bf16[4,2048,256]{2,1,0:T(8,128)(2,1)} %get-tuple-element.76.refs_2_, ...), custom_call_target="tpu_custom_call" | custom-call | flops 12999999488 | bytes 6000000 | tf_op jit(solution)/shard_map/pallas_call | solution.py:45
  140.5 1.8 fusion.refs_10_
  142.4 3.8 %collective-permute-start.24 = (f32[32,2304]{1,0:T(8,128)S(1)}, f32[32,2304]{1,0:T(8,128)S(1)}, u32[]{:S(2)}, u32[]{:S(2)}) collective-permute-start(f32[32,2304]{1,0:T(8,128)S(1)} %get-tuple-element.124), channel_id=1, source_target_pairs={{0,24},{1,25},{2,26},{3,27},{4,28},{5,29},{6,30},{7,31},{8,16},{9,... | collective-permute-start | bytes 884744 | tf_op jit(solution)/shard_map/ppermute | solution.py:712
  146.8 14.2 %shard_map.291 = (bf16[64,2048]{1,0:T(8,128)(2,1)}, bf16[64,2048]{1,0:T(8,128)(2,1)}, bf16[64,2048]{1,0:T(8,128)(2,1)}) custom-call(bf16[256,2048]{1,0:T(8,128)(2,1)} %get-tuple-element.73.refs_0_, bf16[256,2048]{1,0:T(8,128)(2,1)} %get-tuple-element.75.refs_1_, bf16[4,2048,256]{2,1,0:T(8,128)(2,1)} %get-tuple-element.76.refs_2_, ...), custom_call_target="tpu_custom_call" | custom-call | flops 12999999488 | bytes 6000000 | tf_op jit(solution)/shard_map/pallas_call | solution.py:45
  161.7 6.9 %shard_map.292 = (f32[272,768]{1,0:T(8,128)}, f32[272,768]{1,0:T(8,128)}) custom-call(s32[16]{0:T(128)} %get-tuple-element.133.refs_0_, bf16[512,2048]{1,0:T(8,128)(2,1)} %get-tuple-element.102.refs_1_, f32[8,2048]{1,0:T(8,128)} %get-tuple-element.74.refs_5_.refs_2_, f32[8,2048]{1,0:T(8,128)} %copy-done.18, ...), custom_call_target="tpu_custom_call" | custom-call | flops 4000000000 | bytes 8000000 | tf_op jit(solution)/shard_map/pallas_call | solution.py:45
  169.0 1.7 collective-permute-done.26
  170.7 1.0 constant_dynamic-update-slice_fusion.9
  171.7 2.5 collective-permute-start.29
  174.2 1.9 collective-permute-start.27
  176.1 5.2 %shard_map.293 = (f32[512,1024]{1,0:T(8,128)}, f32[512,1024]{1,0:T(8,128)}) custom-call(bf16[3,512,256]{2,1,0:T(8,128)(2,1)} %refs_0_.3, bf16[64,2048]{1,0:T(8,128)(2,1)} %get-tuple-element.89.refs_4_.refs_1_, bf16[64,2048]{1,0:T(8,128)(2,1)} %get-tuple-element.90.refs_5_.refs_2_, bf16[64,2048]{1,0:T(8,128)(2,1)} %get-tuple-element.92.refs_6_.refs_3_, ...), custom_call_target="tpu_custom_call" | custom-call | flops 4000000000 | bytes 8000000 | tf_op jit(solution)/shard_map/pallas_call | solution.py:45
  181.3 2.2 collective-permute-done.29
  183.5 7.6 %collective-permute-done.28 = f32[32,2304]{1,0:T(8,128)S(1)} collective-permute-done((f32[32,2304]{1,0:T(8,128)S(1)}, f32[32,2304]{1,0:T(8,128)S(1)}, u32[]{:S(2)}, u32[]{:S(2)}) %collective-permute-start.28) | collective-permute-done | bytes 294944 | tf_op jit(solution)/shard_map/ppermute | solution.py:712
  191.1 6.2 %collective-permute-done.27 = f32[32,2304]{1,0:T(8,128)S(1)} collective-permute-done((f32[32,2304]{1,0:T(8,128)S(1)}, f32[32,2304]{1,0:T(8,128)S(1)}, u32[]{:S(2)}, u32[]{:S(2)}) %collective-permute-start.27) | collective-permute-done | bytes 294944 | tf_op jit(solution)/shard_map/ppermute | solution.py:712
  197.4 1.6 collective-permute-start.30
  199.0 1.1 slice_add_fusion.2
  200.7 17.7 %collective-permute-done.15 = f32[144,768]{1,0:T(8,128)S(1)} collective-permute-done((f32[144,768]{1,0:T(8,128)S(1)}, f32[144,768]{1,0:T(8,128)S(1)}, u32[]{:S(2)}, u32[]{:S(2)}) %collective-permute-start.15) | collective-permute-done | bytes 442400 | tf_op jit(solution)/shard_map/ppermute | solution.py:712
  218.4 1.1 slice_add_fusion.3
  219.6 2.1 collective-permute-start.31
  221.7 1.7 collective-permute-start.16
  223.4 4.9 %shard_map.294.refs_1_ = f32[1024,512]{1,0:T(8,128)} custom-call(f32[512,1024]{1,0:T(8,128)} %get-tuple-element.104.refs_0_, f32[512,1024]{1,0:T(8,128)} %collective-permute-done.12.refs_1_, f32[1024,512]{1,0:T(8,128)} %get-tuple-element.106.refs_2_), custom_call_target="tpu_custom_call" | custom-call | bytes 8000000 | tf_op jit(solution)/shard_map/pallas_call | solution.py:45
  228.7 2.4 collective-permute-start.18
  231.1 6.2 %collective-permute-done.17 = f32[48,768]{1,0:T(8,128)S(1)} collective-permute-done((f32[48,768]{1,0:T(8,128)S(1)}, f32[48,768]{1,0:T(8,128)S(1)}, u32[]{:S(2)}, u32[]{:S(2)}) %collective-permute-start.17) | collective-permute-done | bytes 147488 | tf_op jit(solution)/shard_map/ppermute | solution.py:712
  237.3 1.4 collective-permute-done.18
  238.7 2.2 collective-permute-start.21
  240.9 4.3 %collective-permute-done.21 = f32[32,768]{1,0:T(8,128)S(1)} collective-permute-done((f32[32,768]{1,0:T(8,128)S(1)}, f32[32,768]{1,0:T(8,128)S(1)}, u32[]{:S(2)}, u32[]{:S(2)}) %collective-permute-start.21) | collective-permute-done | bytes 98336 | tf_op jit(solution)/shard_map/ppermute | solution.py:712
  245.3 1.7 collective-permute-done.20
  247.0 4.8 %collective-permute-done.19 = f32[32,768]{1,0:T(8,128)S(1)} collective-permute-done((f32[32,768]{1,0:T(8,128)S(1)}, f32[32,768]{1,0:T(8,128)S(1)}, u32[]{:S(2)}, u32[]{:S(2)}) %collective-permute-start.19) | collective-permute-done | bytes 98336 | tf_op jit(solution)/shard_map/ppermute | solution.py:712
  251.9 1.5 collective-permute-start.22
  253.5 7.2 %collective-permute-done.22 = f32[128,768]{1,0:T(8,128)S(1)} collective-permute-done((f32[128,768]{1,0:T(8,128)S(1)}, f32[128,768]{1,0:T(8,128)S(1)}, u32[]{:S(2)}, u32[]{:S(2)}) %collective-permute-start.22) | collective-permute-done | bytes 393248 | tf_op jit(solution)/shard_map/ppermute | solution.py:712
  261.2 3.6 %shard_map.284 = bf16[2048,512]{1,0:T(8,128)(2,1)} custom-call(s32[1]{0:T(128)} %bitcast.refs_0_.refs_1_, f32[1024,512]{1,0:T(8,128)} %get-tuple-element.72.refs_1_, f32[1024,512]{1,0:T(8,128)} %collective-permute-done.5.refs_2_), custom_call_target="tpu_custom_call" | custom-call | bytes 6000000 | tf_op jit(solution)/shard_map/pallas_call | solution.py:45
  265.5 7.4 %collective-permute-done.23.refs_2_ = f32[256,768]{1,0:T(8,128)} collective-permute-done((f32[256,768]{1,0:T(8,128)S(1)}, f32[256,768]{1,0:T(8,128)}, u32[]{:S(2)}, u32[]{:S(2)}) %collective-permute-start.23) | collective-permute-done | bytes 786464 | tf_op jit(solution)/shard_map/ppermute | solution.py:712
  272.9 3.3 %shard_map.296 = (f32[3,512,256]{2,1,0:T(8,128)}, f32[2,256]{1,0:T(2,128)}, f32[1,1024]{1,0:T(1,128)}, f32[1,512]{1,0:T(1,128)}, f32[1,512]{1,0:T(1,128)}, /*ind...) custom-call(s32[16]{0:T(128)} %get-tuple-element.133.refs_0_, f32[256,768]{1,0:T(8,128)} %copy-done.5, ...), custom_call_target="tpu_custom_call" | custom-call | bytes 6000000 | tf_op jit(solution)/shard_map/pallas_call | solution.py:45
  276.2 6.0 %shard_map.297 = (f32[1024,512]{1,0:T(8,128)}, f32[512,1024]{1,0:T(8,128)}, f32[256,512]{1,0:T(8,128)}) custom-call(s32[16]{0:T(128)} %get-tuple-element.133.refs_0_, f32[256,2304]{1,0:T(8,128)} %copy-done.2, f32[256,2304]{1,0:T(8,128)} %collective-permute-done.31.refs_2_), custom_call_target="tpu_custom_call" | custom-call | bytes 10000000 | tf_op jit(solution)/shard_map/pallas_call | solution.py:45
  282.1 3.6 %shard_map.295 = bf16[2048,512]{1,0:T(8,128)(2,1)} custom-call(s32[1]{0:T(128)} %bitcast.refs_0_.refs_1_, f32[1024,512]{1,0:T(8,128)} %shard_map.294.refs_1_, f32[1024,512]{1,0:T(8,128)} %collective-permute-done.13.refs_2_), custom_call_target="tpu_custom_call" | custom-call | bytes 6000000 | tf_op jit(solution)/shard_map/pallas_call | solution.py:45
  (103 shorter events, 11.3 us)
Async XLA Ops:
  0.6 4.5 %copy-start.14 = (s32[1,16]{1,0:T(1,128)S(1)}, s32[1,16]{1,0:T(1,128)}, u32[]{:S(2)}) copy-start(s32[1,16]{1,0:T(1,128)} %param.19) | copy-start | bytes 196
  0.7 4.5 %copy-start.21 = (s32[1,16]{1,0:T(1,128)S(1)}, s32[1,16]{1,0:T(1,128)}, u32[]{:S(2)}) copy-start(s32[1,16]{1,0:T(1,128)} %param.20) | copy-start | bytes 196
  4.6 30.7 %collective-permute-start.2 = (f32[512,1024]{1,0:T(8,128)}, f32[512,1024]{1,0:T(8,128)S(1)}, u32[]{:S(2)}, u32[]{:S(2)}) collective-permute-start(f32[512,1024]{1,0:T(8,128)} %get-tuple-element.70), channel_id=1, source_target_pairs={{0,1},{1,0},{2,3},{3,2},{4,5},{5,4},{6,7},{7,6},{8,9},{9,8},{10,11... | collective-permute-start | bytes 6291464 | tf_op jit(solution)/shard_map/ppermute | solution.py:692
  5.1 30.2 %collective-permute-start.3 = (f32[1024,512]{1,0:T(8,128)}, f32[1024,512]{1,0:T(8,128)}, u32[]{:S(2)}, u32[]{:S(2)}) collective-permute-start(f32[1024,512]{1,0:T(8,128)} %get-tuple-element.71), channel_id=1, source_target_pairs={{0,1},{1,0},{2,3},{3,2},{4,5},{5,4},{6,7},{7,6},{8,9},{9,8},{10,11... | collective-permute-start | bytes 6291464 | tf_op jit(solution)/shard_map/ppermute | solution.py:692
  5.7 26.3 %copy-start.19 = (f32[1024]{0:T(1024)S(1)}, f32[1024]{0:T(1024)}, u32[]{:S(2)}) copy-start(f32[1024]{0:T(1024)} %param.28) | copy-start | bytes 12292
  5.8 26.7 %copy-start.13 = (s32[2,16]{1,0:T(2,128)S(1)}, s32[2,16]{1,0:T(2,128)}, u32[]{:S(2)}) copy-start(s32[2,16]{1,0:T(2,128)} %constant.18.clone) | copy-start | bytes 388
  5.8 27.3 %copy-start.7 = (f32[512]{0:T(512)S(1)}, f32[512]{0:T(512)}, u32[]{:S(2)}) copy-start(f32[512]{0:T(512)} %param.25) | copy-start | bytes 6148
  5.8 27.3 %copy-start.8 = (f32[512]{0:T(512)S(1)}, f32[512]{0:T(512)}, u32[]{:S(2)}) copy-start(f32[512]{0:T(512)} %param.24) | copy-start | bytes 6148
  5.8 27.3 %copy-start.9 = (f32[512]{0:T(512)S(1)}, f32[512]{0:T(512)}, u32[]{:S(2)}) copy-start(f32[512]{0:T(512)} %param.26) | copy-start | bytes 6148
  5.8 27.3 %copy-start.10 = (f32[512]{0:T(512)S(1)}, f32[512]{0:T(512)}, u32[]{:S(2)}) copy-start(f32[512]{0:T(512)} %param.30) | copy-start | bytes 6148
  5.8 27.3 %copy-start.11 = (f32[512]{0:T(512)S(1)}, f32[512]{0:T(512)}, u32[]{:S(2)}) copy-start(f32[512]{0:T(512)} %param.31) | copy-start | bytes 6148
  5.8 27.3 %copy-start.12 = (f32[512]{0:T(512)S(1)}, f32[512]{0:T(512)}, u32[]{:S(2)}) copy-start(f32[512]{0:T(512)} %param.32) | copy-start | bytes 6148
  31.5 3.8 %collective-permute-start = (f32[256,1024]{1,0:T(8,128)}, f32[256,1024]{1,0:T(8,128)S(1)}, u32[]{:S(2)}, u32[]{:S(2)}) collective-permute-start(f32[256,1024]{1,0:T(8,128)} %get-tuple-element.68.refs_6_), channel_id=1, source_target_pairs={{0,1},{1,0},{2,3},{3,2},{4,5},{5,4},{6,7},{7,6},{8,9},{9,8},{10,11... | collective-permute-start | bytes 3145736 | tf_op jit(solution)/shard_map/ppermute | solution.py:692
  32.0 3.3 %collective-permute-start.1 = (f32[256,512]{1,0:T(8,128)}, f32[256,512]{1,0:T(8,128)}, u32[]{:S(2)}, u32[]{:S(2)}) collective-permute-start(f32[256,512]{1,0:T(8,128)} %get-tuple-element.69), channel_id=1, source_target_pairs={{0,1},{1,0},{2,3},{3,2},{4,5},{5,4},{6,7},{7,6},{8,9},{9,8},{10,11... | collective-permute-start | bytes 1572872 | tf_op jit(solution)/shard_map/ppermute | solution.py:692
  32.0 2.9 %collective-permute-start.4 = (f32[1,1024]{1,0:T(1,128)S(1)}, f32[1,1024]{1,0:T(1,128)S(1)}, u32[]{:S(2)}, u32[]{:S(2)}) collective-permute-start(f32[1,1024]{1,0:T(1,128)S(1)} %bitcast.28), channel_id=1, source_target_pairs={{0,1},{1,0},{2,3},{3,2},{4,5},{5,4},{6,7},{7,6},{8,9},{9,8},{10,11... | collective-permute-start | bytes 12296 | tf_op jit(solution)/shard_map/ppermute | solution.py:692
  68.6 7.0 %collective-permute-start.8 = (f32[256,2304]{1,0:T(8,128)}, f32[256,2304]{1,0:T(8,128)}, u32[]{:S(2)}, u32[]{:S(2)}) collective-permute-start(f32[256,2304]{1,0:T(8,128)} %get-tuple-element.91), channel_id=1, source_target_pairs={{0,1},{1,0},{2,3},{3,2},{4,5},{5,4},{6,7},{7,6},{8,9},{9,8},{10,11... | collective-permute-start | bytes 7077896 | tf_op jit(solution)/shard_map/ppermute | solution.py:692
  69.0 15.9 %collective-permute-start.7 = (f32[256,2304]{1,0:T(8,128)}, f32[256,2304]{1,0:T(8,128)S(1)}, u32[]{:S(2)}, u32[]{:S(2)}) collective-permute-start(f32[256,2304]{1,0:T(8,128)} %get-tuple-element.88), channel_id=1, source_target_pairs={{0,1},{1,0},{2,3},{3,2},{4,5},{5,4},{6,7},{7,6},{8,9},{9,8},{10,11... | collective-permute-start | bytes 7077896 | tf_op jit(solution)/shard_map/ppermute | solution.py:692
  69.2 23.9 %collective-permute-start.6 = (f32[256,1024]{1,0:T(8,128)}, f32[256,1024]{1,0:T(8,128)S(1)}, u32[]{:S(2)}, u32[]{:S(2)}) collective-permute-start(f32[256,1024]{1,0:T(8,128)} %get-tuple-element.80), channel_id=1, source_target_pairs={{0,1},{1,0},{2,3},{3,2},{4,5},{5,4},{6,7},{7,6},{8,9},{9,8},{10,11... | collective-permute-start | bytes 3145736 | tf_op jit(solution)/shard_map/ppermute | solution.py:692
  69.5 91.5 %collective-permute-start.11 = (f32[8,2048]{1,0:T(8,128)}, f32[8,2048]{1,0:T(8,128)S(1)}, u32[]{:S(2)}, u32[]{:S(2)}) collective-permute-start(f32[8,2048]{1,0:T(8,128)} %get-tuple-element.74.refs_5_.refs_2_), channel_id=1, source_target_pairs={{0,1},{1,0},{2,3},{3,2},{4,5},{5,4},{6,7},{7,6},{8,9},{9,8},{10,11... | collective-permute-start | bytes 196616 | tf_op jit(solution)/shard_map/ppermute | solution.py:692
  69.7 191.5 %collective-permute-start.5 = (f32[1024,512]{1,0:T(8,128)}, f32[1024,512]{1,0:T(8,128)}, u32[]{:S(2)}, u32[]{:S(2)}) collective-permute-start(f32[1024,512]{1,0:T(8,128)} %get-tuple-element.72.refs_1_), channel_id=1, source_target_pairs={{0,1},{1,0},{2,3},{3,2},{4,5},{5,4},{6,7},{7,6},{8,9},{9,8},{10,11... | collective-permute-start | bytes 6291464 | tf_op jit(solution)/shard_map/ppermute | solution.py:692
  82.2 40.5 %collective-permute-start.9 = (f32[256,2304]{1,0:T(8,128)}, f32[256,2304]{1,0:T(8,128)}, u32[]{:S(2)}, u32[]{:S(2)}) collective-permute-start(f32[256,2304]{1,0:T(8,128)} %shard_map.289), channel_id=1, source_target_pairs={{0,2},{1,5},{2,0},{3,7},{4,6},{5,1},{6,4},{7,3},{8,10},{9,13},{10,... | collective-permute-start | bytes 7077896 | tf_op jit(solution)/shard_map/ppermute | solution.py:712
  108.4 14.3 %copy-start = (f32[256,2304]{1,0:T(8,128)S(1)}, f32[256,2304]{1,0:T(8,128)}, u32[]{:S(2)}) copy-start(f32[256,2304]{1,0:T(8,128)} %shard_map.286.refs_10_) | copy-start | bytes 7077892
  124.1 1.7 copy-start.4
  124.1 16.4 %collective-permute-start.10 = (f32[128,2304]{1,0:T(8,128)S(1)}, f32[128,2304]{1,0:T(8,128)}, u32[]{:S(2)}, u32[]{:S(2)}) collective-permute-start(f32[128,2304]{1,0:T(8,128)S(1)} %slice_add_fusion.1.refs_10_), channel_id=1, source_target_pairs={{0,4},{1,3},{2,6},{3,1},{4,0},{5,7},{6,2},{7,5},{8,12},{9,11},{10,... | collective-permute-start | bytes 3538952 | tf_op jit(solution)/shard_map/ppermute | solution.py:712
  142.3 4.5 %copy-start.1 = (f32[128,2304]{1,0:T(8,128)}, f32[128,2304]{1,0:T(8,128)S(1)}, u32[]{:S(2)}) copy-start(f32[128,2304]{1,0:T(8,128)S(1)} %fusion.refs_10_) | copy-start | bytes 3538948
  142.4 26.6 %collective-permute-start.24 = (f32[32,2304]{1,0:T(8,128)S(1)}, f32[32,2304]{1,0:T(8,128)S(1)}, u32[]{:S(2)}, u32[]{:S(2)}) collective-permute-start(f32[32,2304]{1,0:T(8,128)S(1)} %get-tuple-element.124), channel_id=1, source_target_pairs={{0,24},{1,25},{2,26},{3,27},{4,28},{5,29},{6,30},{7,31},{8,16},{9,... | collective-permute-start | bytes 884744 | tf_op jit(solution)/shard_map/ppermute | solution.py:712
  146.1 24.5 %collective-permute-start.26 = (f32[32,2304]{1,0:T(8,128)S(1)}, f32[32,2304]{1,0:T(8,128)S(1)}, u32[]{:S(2)}, u32[]{:S(2)}) collective-permute-start(f32[32,2304]{1,0:T(8,128)S(1)} %get-tuple-element.125), channel_id=1, source_target_pairs={{0,16},{1,17},{2,18},{3,19},{4,20},{5,21},{6,22},{7,23},{8,24},{9,... | collective-permute-start | bytes 884744 | tf_op jit(solution)/shard_map/ppermute | solution.py:712
  146.1 24.5 %collective-permute-start.25 = (f32[32,2304]{1,0:T(8,128)S(1)}, f32[32,2304]{1,0:T(8,128)S(1)}, u32[]{:S(2)}, u32[]{:S(2)}) collective-permute-start(f32[32,2304]{1,0:T(8,128)S(1)} %get-tuple-element.126), channel_id=1, source_target_pairs={{0,8},{1,9},{2,10},{3,11},{4,12},{5,13},{6,14},{7,15},{8,0},{9,1},... | collective-permute-start | bytes 884744 | tf_op jit(solution)/shard_map/ppermute | solution.py:712
  168.6 30.4 %collective-permute-start.14 = (f32[272,768]{1,0:T(8,128)}, f32[272,768]{1,0:T(8,128)}, u32[]{:S(2)}, u32[]{:S(2)}) collective-permute-start(f32[272,768]{1,0:T(8,128)} %get-tuple-element.107), channel_id=1, source_target_pairs={{0,2},{1,5},{2,0},{3,7},{4,6},{5,1},{6,4},{7,3},{8,10},{9,13},{10,... | collective-permute-start | bytes 2506760 | tf_op jit(solution)/shard_map/ppermute | solution.py:712
  171.7 11.8 %collective-permute-start.29 = (f32[32,2304]{1,0:T(8,128)S(1)}, f32[32,2304]{1,0:T(8,128)S(1)}, u32[]{:S(2)}, u32[]{:S(2)}) collective-permute-start(f32[32,2304]{1,0:T(8,128)S(1)} %get-tuple-element.121), channel_id=1, source_target_pairs={{0,24},{1,25},{2,26},{3,27},{4,28},{5,29},{6,30},{7,31},{8,16},{9,... | collective-permute-start | bytes 884744 | tf_op jit(solution)/shard_map/ppermute | solution.py:712
  174.2 16.8 %collective-permute-start.28 = (f32[32,2304]{1,0:T(8,128)S(1)}, f32[32,2304]{1,0:T(8,128)S(1)}, u32[]{:S(2)}, u32[]{:S(2)}) collective-permute-start(f32[32,2304]{1,0:T(8,128)S(1)} %get-tuple-element.121), channel_id=1, source_target_pairs={{0,8},{1,9},{2,10},{3,11},{4,12},{5,13},{6,14},{7,15},{8,0},{9,1},... | collective-permute-start | bytes 884744 | tf_op jit(solution)/shard_map/ppermute | solution.py:712
  174.2 23.0 %collective-permute-start.27 = (f32[32,2304]{1,0:T(8,128)S(1)}, f32[32,2304]{1,0:T(8,128)S(1)}, u32[]{:S(2)}, u32[]{:S(2)}) collective-permute-start(f32[32,2304]{1,0:T(8,128)S(1)} %get-tuple-element.121), channel_id=1, source_target_pairs={{0,16},{1,17},{2,18},{3,19},{4,20},{5,21},{6,22},{7,23},{8,24},{9,... | collective-permute-start | bytes 884744 | tf_op jit(solution)/shard_map/ppermute | solution.py:712
  181.3 17.7 %copy-start.6 = (f32[272,768]{1,0:T(8,128)S(1)}, f32[272,768]{1,0:T(8,128)}, u32[]{:S(2)}) copy-start(f32[272,768]{1,0:T(8,128)} %get-tuple-element.103.refs_13_) | copy-start | bytes 2506756
  183.5 39.9 %collective-permute-start.12 = (f32[512,1024]{1,0:T(8,128)}, f32[512,1024]{1,0:T(8,128)}, u32[]{:S(2)}, u32[]{:S(2)}) collective-permute-start(f32[512,1024]{1,0:T(8,128)} %get-tuple-element.105), channel_id=1, source_target_pairs={{0,1},{1,0},{2,3},{3,2},{4,5},{5,4},{6,7},{7,6},{8,9},{9,8},{10,11... | collective-permute-start | bytes 6291464 | tf_op jit(solution)/shard_map/ppermute | solution.py:692
  197.4 22.1 %collective-permute-start.30 = (f32[128,2304]{1,0:T(8,128)S(1)}, f32[128,2304]{1,0:T(8,128)S(1)}, u32[]{:S(2)}, u32[]{:S(2)}) collective-permute-start(f32[128,2304]{1,0:T(8,128)S(1)} %pad_maximum_fusion), channel_id=1, source_target_pairs={{0,4},{1,3},{2,6},{3,1},{4,0},{5,7},{6,2},{7,5},{8,12},{9,11},{10,... | collective-permute-start | bytes 3538952 | tf_op jit(solution)/shard_map/ppermute | solution.py:712
  200.1 18.3 %collective-permute-start.15 = (f32[144,768]{1,0:T(8,128)S(1)}, f32[144,768]{1,0:T(8,128)S(1)}, u32[]{:S(2)}, u32[]{:S(2)}) collective-permute-start(f32[144,768]{1,0:T(8,128)S(1)} %slice_add_fusion.2), channel_id=1, source_target_pairs={{0,4},{1,3},{2,6},{3,1},{4,0},{5,7},{6,2},{7,5},{8,12},{9,11},{10,... | collective-permute-start | bytes 1327112 | tf_op jit(solution)/shard_map/ppermute | solution.py:712
  219.6 8.8 %copy-start.2 = (f32[256,2304]{1,0:T(8,128)}, f32[256,2304]{1,0:T(8,128)S(1)}, u32[]{:S(2)}) copy-start(f32[256,2304]{1,0:T(8,128)S(1)} %constant_dynamic-update-slice_fusion.5.refs_1_) | copy-start | bytes 7077892
  219.6 56.6 %collective-permute-start.31 = (f32[256,2304]{1,0:T(8,128)S(1)}, f32[256,2304]{1,0:T(8,128)}, u32[]{:S(2)}, u32[]{:S(2)}) collective-permute-start(f32[256,2304]{1,0:T(8,128)S(1)} %constant_dynamic-update-slice_fusion.5.refs_1_), channel_id=1, source_target_pairs={{0,2},{1,5},{2,0},{3,7},{4,6},{5,1},{6,4},{7,3},{8,10},{9,13},{10,... | collective-permute-start | bytes 7077896 | tf_op jit(solution)/shard_map/ppermute | solution.py:712
  221.7 7.0 %collective-permute-start.16 = (f32[48,768]{1,0:T(8,128)S(1)}, f32[48,768]{1,0:T(8,128)S(1)}, u32[]{:S(2)}, u32[]{:S(2)}) collective-permute-start(f32[48,768]{1,0:T(8,128)S(1)} %get-tuple-element.130), channel_id=1, source_target_pairs={{0,24},{1,25},{2,26},{3,27},{4,28},{5,29},{6,30},{7,31},{8,16},{9,... | collective-permute-start | bytes 442376 | tf_op jit(solution)/shard_map/ppermute | solution.py:712
  228.3 53.8 %collective-permute-start.13 = (f32[1024,512]{1,0:T(8,128)}, f32[1024,512]{1,0:T(8,128)}, u32[]{:S(2)}, u32[]{:S(2)}) collective-permute-start(f32[1024,512]{1,0:T(8,128)} %shard_map.294.refs_1_), channel_id=1, source_target_pairs={{0,1},{1,0},{2,3},{3,2},{4,5},{5,4},{6,7},{7,6},{8,9},{9,8},{10,11... | collective-permute-start | bytes 6291464 | tf_op jit(solution)/shard_map/ppermute | solution.py:692
  228.3 9.0 %collective-permute-start.17 = (f32[48,768]{1,0:T(8,128)S(1)}, f32[48,768]{1,0:T(8,128)S(1)}, u32[]{:S(2)}, u32[]{:S(2)}) collective-permute-start(f32[48,768]{1,0:T(8,128)S(1)} %get-tuple-element.131), channel_id=1, source_target_pairs={{0,8},{1,9},{2,10},{3,11},{4,12},{5,13},{6,14},{7,15},{8,0},{9,1},... | collective-permute-start | bytes 442376 | tf_op jit(solution)/shard_map/ppermute | solution.py:712
  228.7 10.0 %collective-permute-start.18 = (f32[48,768]{1,0:T(8,128)S(1)}, f32[48,768]{1,0:T(8,128)S(1)}, u32[]{:S(2)}, u32[]{:S(2)}) collective-permute-start(f32[48,768]{1,0:T(8,128)S(1)} %get-tuple-element.132), channel_id=1, source_target_pairs={{0,16},{1,17},{2,18},{3,19},{4,20},{5,21},{6,22},{7,23},{8,24},{9,... | collective-permute-start | bytes 442376 | tf_op jit(solution)/shard_map/ppermute | solution.py:712
  238.7 6.6 %collective-permute-start.21 = (f32[32,768]{1,0:T(8,128)S(1)}, f32[32,768]{1,0:T(8,128)S(1)}, u32[]{:S(2)}, u32[]{:S(2)}) collective-permute-start(f32[32,768]{1,0:T(8,128)S(1)} %get-tuple-element.123), channel_id=1, source_target_pairs={{0,24},{1,25},{2,26},{3,27},{4,28},{5,29},{6,30},{7,31},{8,16},{9,... | collective-permute-start | bytes 294920 | tf_op jit(solution)/shard_map/ppermute | solution.py:712
  240.9 6.1 %collective-permute-start.20 = (f32[32,768]{1,0:T(8,128)S(1)}, f32[32,768]{1,0:T(8,128)S(1)}, u32[]{:S(2)}, u32[]{:S(2)}) collective-permute-start(f32[32,768]{1,0:T(8,128)S(1)} %get-tuple-element.123), channel_id=1, source_target_pairs={{0,8},{1,9},{2,10},{3,11},{4,12},{5,13},{6,14},{7,15},{8,0},{9,1},... | collective-permute-start | bytes 294920 | tf_op jit(solution)/shard_map/ppermute | solution.py:712
  245.3 6.6 %collective-permute-start.19 = (f32[32,768]{1,0:T(8,128)S(1)}, f32[32,768]{1,0:T(8,128)S(1)}, u32[]{:S(2)}, u32[]{:S(2)}) collective-permute-start(f32[32,768]{1,0:T(8,128)S(1)} %get-tuple-element.123), channel_id=1, source_target_pairs={{0,16},{1,17},{2,18},{3,19},{4,20},{5,21},{6,22},{7,23},{8,24},{9,... | collective-permute-start | bytes 294920 | tf_op jit(solution)/shard_map/ppermute | solution.py:712
  251.9 8.8 %collective-permute-start.22 = (f32[128,768]{1,0:T(8,128)S(1)}, f32[128,768]{1,0:T(8,128)S(1)}, u32[]{:S(2)}, u32[]{:S(2)}) collective-permute-start(f32[128,768]{1,0:T(8,128)S(1)} %pad_maximum_fusion.1), channel_id=1, source_target_pairs={{0,4},{1,3},{2,6},{3,1},{4,0},{5,7},{6,2},{7,5},{8,12},{9,11},{10,... | collective-permute-start | bytes 1179656 | tf_op jit(solution)/shard_map/ppermute | solution.py:712
  260.7 4.2 %copy-start.5 = (f32[256,768]{1,0:T(8,128)}, f32[256,768]{1,0:T(8,128)S(1)}, u32[]{:S(2)}) copy-start(f32[256,768]{1,0:T(8,128)S(1)} %constant_dynamic-update-slice_fusion.refs_1_) | copy-start | bytes 2359300
  260.7 12.2 %collective-permute-start.23 = (f32[256,768]{1,0:T(8,128)S(1)}, f32[256,768]{1,0:T(8,128)}, u32[]{:S(2)}, u32[]{:S(2)}) collective-permute-start(f32[256,768]{1,0:T(8,128)S(1)} %constant_dynamic-update-slice_fusion.refs_1_), channel_id=1, source_target_pairs={{0,2},{1,5},{2,0},{3,7},{4,6},{5,1},{6,4},{7,3},{8,10},{9,13},{10,... | collective-permute-start | bytes 2359304 | tf_op jit(solution)/shard_map/ppermute | solution.py:712
  (6 other events, 6.2 us)
